TPU v7x, 128 devices: a whole 4x4x4 slice. The times are simulated.
128 devices in a mesh: gx: 8 (over y, core), gy: 16 (over z, x).
Axes of the slice: x: 4, y: 4, z: 4, core: 2. Of those that a mesh axis runs over, the one named last changes fastest.
Arguments:
- pixels: int32 [32, 32, 4, 131072], P('gy', 'gx'), may hold values from 0 to 255, as said below
- weights: bfloat16 [32, 32, 4, 131072], P('gy', 'gx'), may hold values from 0.25 to 1
- adjacency: int32 [2, 32, 32], replicated, may hold values 0 or 1
Outputs:
- log_gain: float32 [32, 32], P('gy', 'gx')
Inputs may be any that keep to these rules, and one draw needn't show every extreme that they name: `pixels`: bin indices of 8-bit intensities. `adjacency`: entry [0, r, c] is 1 where tile (r, c) and the tile to its right share a usable border, entry [1, r, c] likewise for the tile below; entries of pairs beyond the grid's edge are read by no output.
All inputs are finite; a program needn't handle non-finite values.
Results may differ from a plain program's by a relative error of at most 0.0003.
Values may be sent and summed in bfloat16 or wider, within the bound.
No kernel may reach another device: no remote copies, remote signals or barrier semaphores. Data moves between devices by JAX's collectives and lax.ppermute only.
A program may use at most 128 MiB of HBM per device.

v0:
```python
import functools

import jax
import jax.numpy as jnp
import numpy as np
from jax import lax
from jax.experimental import pallas as pl
from jax.experimental.pallas import tpu as pltpu
from jax.sharding import PartitionSpec as P

ITERS = 20
ROWS, COLS = 2, 4
CHUNKS, LANES = 1024, 128
LINES = 4 * CHUNKS
GROUP = 16
ALL = ("gx", "gy")
F32, BF16, I32 = jnp.float32, jnp.bfloat16, jnp.int32
VMEM_BYTES = 56 << 20

anchor_weight = 0.5
mismatch_scale = 8.0

INNER = np.array(
    [(c, 1, 4 + c, 0) for c in range(4)]
    + [(4 * r + c, 3, 4 * r + c + 1, 2) for r in range(2) for c in range(3)],
    np.int32,
)
OUTER = np.array([(4, 1), (5, 1), (2, 0), (3, 0), (0, 2), (4, 2)], np.int32)


def by_lines(array):
    tiles = array.reshape(ROWS * COLS, 4, CHUNKS, LANES)
    return tiles.transpose(0, 2, 1, 3).reshape(ROWS * COLS, LINES, LANES)


def pack_kernel(side, lines, px_ref, w_ref, out_ref, wide):
    count = lines // 4
    out_ref[0, 0] = px_ref[0, pl.ds(side, count, stride=4), :].astype(F32).astype(BF16)
    wide[...] = w_ref[0].astype(F32)
    out_ref[0, 1] = wide[pl.ds(side, count, stride=4), :].astype(BF16)


def packed(px, w, first, step, side):
    lines = 1024
    return pl.pallas_call(
        functools.partial(pack_kernel, side, lines),
        grid=(2, LINES // lines),
        in_specs=[
            pl.BlockSpec((1, lines, LANES), lambda n, k: (first + step * n, k, 0)),
            pl.BlockSpec((1, lines, LANES), lambda n, k: (first + step * n, k, 0)),
        ],
        out_specs=pl.BlockSpec((1, 2, lines // 4, LANES), lambda n, k: (n, 0, k, 0)),
        out_shape=jax.ShapeDtypeStruct((2, 2, CHUNKS, LANES), BF16),
        scratch_shapes=[pltpu.VMEM((lines, LANES), F32)],
        compiler_params=pltpu.CompilerParams(vmem_limit_bytes=VMEM_BYTES),
        cost_estimate=pl.CostEstimate(flops=1 << 20, bytes_accessed=7 << 20, transcendentals=0),
    )(px, w)


def one_hot_pair(bins, joint):
    upper = lax.shift_right_logical(bins, 4).astype(F32).astype(BF16)
    lower = (bins & 15).astype(F32).astype(BF16)
    zero, one = jnp.zeros((), BF16), jnp.ones((), BF16)
    left = [jnp.where(upper == BF16(k), joint, zero) for k in range(16)]
    right = [jnp.where(lower == BF16(k), one, zero) for k in range(16)]
    return jnp.concatenate(left, 0), jnp.concatenate(right, 0)


def diagonal_sum(left, right):
    product = lax.dot_general(
        jnp.concatenate(left, 1),
        jnp.concatenate(right, 1),
        (((1,), (1,)), ((), ())),
        preferred_element_type=F32,
    )
    column = lax.broadcasted_iota(I32, (GROUP, 256), 1) % GROUP
    row = lax.broadcasted_iota(I32, (GROUP, 256), 0)
    kept = jnp.where((column == row)[None], product.reshape(16, GROUP, 256), 0.0)
    return jnp.sum(kept, axis=1)


def inner_kernel(table, px_a, px_b, w_a, w_b, out_ref, wide_a, wide_b):
    n = pl.program_id(0)
    side_a, side_b = table[n, 1], table[n, 3]
    ops_a, ops_b = [], []
    for v in range(CHUNKS // GROUP):
        o = 4 * GROUP * v
        wide_a[o : o + 64] = w_a[0, o : o + 64].astype(F32)
        wide_b[o : o + 64] = w_b[0, o : o + 64].astype(F32)
        rows_a = pl.ds(o + side_a, GROUP, stride=4)
        rows_b = pl.ds(o + side_b, GROUP, stride=4)
        joint = (wide_a[rows_a, :] * wide_b[rows_b, :]).astype(BF16)
        ops_a.append(one_hot_pair(px_a[0, rows_a, :], joint))
        ops_b.append(one_hot_pair(px_b[0, rows_b, :], joint))
    for place, ops in enumerate((ops_a, ops_b)):
        out_ref[0, place] = diagonal_sum(*zip(*ops))


def inner_sums(px, w):
    count = len(INNER)
    tile = lambda which: pl.BlockSpec((1, LINES, LANES), lambda n, t: (t[n, which], 0, 0))
    return pl.pallas_call(
        inner_kernel,
        grid_spec=pltpu.PrefetchScalarGridSpec(
            num_scalar_prefetch=1,
            grid=(count,),
            in_specs=[tile(0), tile(2), tile(0), tile(2)],
            out_specs=pl.BlockSpec((1, 2, 16, 256), lambda n, t: (n, 0, 0, 0)),
            scratch_shapes=[pltpu.VMEM((LINES, LANES), F32)] * 2,
        ),
        out_shape=jax.ShapeDtypeStruct((count, 2, 16, 256), F32),
        compiler_params=pltpu.CompilerParams(vmem_limit_bytes=VMEM_BYTES),
        cost_estimate=pl.CostEstimate(
            flops=count * 2 * 2 * 256 * 256 * 8192, bytes_accessed=count * (6 << 20), transcendentals=0
        ),
    )(jnp.asarray(INNER), px, px, w, w)


def f32_dot(a, b):
    return jnp.dot(a, b, precision=lax.Precision.HIGHEST, preferred_element_type=F32)


def pair_results(first, second):
    lower = lax.broadcasted_iota(I32, (256, 384), 0) // GROUP
    column = lax.broadcasted_iota(I32, (256, 384), 1)
    within = ((column < 16) & (lower <= column)) | ((column >= 128) & (column < 256))
    maps = jnp.where(column >= 256, lower.astype(F32) + 0.5, within.astype(F32))
    by_first, by_second = f32_dot(first, maps), f32_dot(second, maps)
    row = lax.broadcasted_iota(I32, (256, 256), 0)
    other = lax.broadcasted_iota(I32, (256, 256), 1)
    same_pair = row // 16 == other // 16
    all_of_pair = same_pair.astype(F32)
    before = (same_pair & (other < row)).astype(F32)
    base = (lax.broadcasted_iota(I32, (256, 128), 0) % 16 * 16).astype(F32)
    total_first = by_first[:, 128:256]
    difference = by_first - by_second
    cumulative = difference[:, :128] + f32_dot(before, difference[:, 128:256])
    moment_first = by_first[:, 256:] + base * total_first
    moment_second = by_second[:, 256:] + base * by_second[:, 128:256]
    lane = lax.broadcasted_iota(I32, (256, 128), 1)
    parts = jnp.concatenate(
        [total_first, moment_first, moment_second, jnp.where(lane < 16, jnp.abs(cumulative), 0.0)], 1
    )
    sums = f32_dot(all_of_pair, parts)
    total = sums[:, :128]
    mean_first, mean_second = sums[:, 128:256] / total, sums[:, 256:384] / total
    distance = jnp.sum(sums[:, 384:], axis=1, keepdims=True) / total
    mismatch = (distance - jnp.abs(mean_first - mean_second)) / mismatch_scale
    confidence = 1.0 / (0.25 + mismatch * mismatch)
    offset = jnp.log(mean_second) - jnp.log(mean_first)
    mine = lax.broadcasted_iota(I32, (256, 128), 0)
    spread = jnp.where(mine == 16 * lane, confidence, jnp.where(mine == 16 * (lane - 16), offset, 0.0))
    spread = jnp.where(total > 0, spread, 0.0)
    return jnp.sum(spread, axis=0, keepdims=True)


def outer_kernel(table, px_ref, w_ref, below, above, left, inner, out_ref, wide, firsts, seconds):
    n = pl.program_id(0)
    side = table[n, 1]
    ops_own, ops_far = [], []
    for v in range(CHUNKS // GROUP):
        o = 4 * GROUP * v
        wide[o : o + 64] = w_ref[0, o : o + 64].astype(F32)
        rows = pl.ds(o + side, GROUP, stride=4)
        dense = slice(GROUP * v, GROUP * (v + 1))

        def far(k):
            return jnp.where(
                n < 2, below[0, k, dense], jnp.where(n < 4, above[0, k, dense], left[0, k, dense])
            )

        joint = (wide[rows, :] * far(1).astype(F32)).astype(BF16)
        ops_own.append(one_hot_pair(px_ref[0, rows, :], joint))
        ops_far.append(one_hot_pair(far(0).astype(F32).astype(I32), joint))
    own, other = diagonal_sum(*zip(*ops_own)), diagonal_sum(*zip(*ops_far))
    done = len(INNER)
    place = pl.ds(pl.multiple_of((done + n) * 16, 16), 16)
    firsts[place, :] = jnp.where(n < 2, own, other)
    seconds[place, :] = jnp.where(n < 2, other, own)

    @pl.when(n == len(OUTER) - 1)
    def _():
        firsts[: done * 16] = inner[:, 0].reshape(done * 16, 256)
        seconds[: done * 16] = inner[:, 1].reshape(done * 16, 256)
        out_ref[...] = jnp.broadcast_to(pair_results(firsts[...], seconds[...]), out_ref.shape)


def outer_results(px, w, below, above, left, inner, devices):
    count = len(OUTER)
    tile = pl.BlockSpec((1, LINES, LANES), lambda n, t: (t[n, 0], 0, 0))
    strip = lambda low: pl.BlockSpec(
        (1, 2, CHUNKS, LANES), lambda n, t: (jnp.clip(n - low, 0, 1), 0, 0, 0)
    )
    return pl.pallas_call(
        outer_kernel,
        grid_spec=pltpu.PrefetchScalarGridSpec(
            num_scalar_prefetch=1,
            grid=(count,),
            in_specs=[
                tile, tile, strip(0), strip(2), strip(4),
                pl.BlockSpec(inner.shape, lambda n, t: (0, 0, 0, 0)),
            ],
            out_specs=pl.BlockSpec((devices, LANES), lambda n, t: (0, 0)),
            scratch_shapes=[
                pltpu.VMEM((LINES, LANES), F32),
                pltpu.VMEM((256, 256), F32),
                pltpu.VMEM((256, 256), F32),
            ],
        ),
        out_shape=jax.ShapeDtypeStruct((devices, LANES), F32),
        compiler_params=pltpu.CompilerParams(vmem_limit_bytes=VMEM_BYTES),
        cost_estimate=pl.CostEstimate(
            flops=count * 2 * 2 * 256 * 256 * 8192, bytes_accessed=count * (4 << 20), transcendentals=0
        ),
    )(jnp.asarray(OUTER), px, w, below, above, left, inner)


def on_grid(gathered, height, count_y):
    devices = gathered.shape[0]
    slot = lax.broadcasted_iota(I32, (LANES, LANES), 0)
    lane = lax.broadcasted_iota(I32, (LANES, LANES), 1)
    c, odd, right = lane % 4, lane // 32 % 2, lane // 64 == 1
    offset_slots = 16 * odd
    edge = right & (c == 3)
    slots = [
        jnp.where(edge, 14, jnp.where(right, 4 + c, c)),
        jnp.where(edge, 15, jnp.where(right, 7 + c, jnp.where(c < 2, 10 + c, -100))),
        jnp.where(right | (c < 2), -100, 10 + c),
    ]
    choose = jnp.concatenate([(slot == s + offset_slots).astype(F32) for s in slots], 1)
    chosen = f32_dot(gathered, choose)
    device = lax.broadcasted_iota(I32, (devices, LANES), 0)
    lane = lax.broadcasted_iota(I32, (devices, LANES), 1)
    shifted = ((lane // 64 == 1) & (lane % 4 == 3)).astype(I32)
    here = device // count_y == lane % 32 // 4 + shifted
    parts = [jnp.where(here, chosen[:, LANES * k : LANES * (k + 1)], 0.0) for k in range(3)]
    row = lax.broadcasted_iota(I32, (height, devices), 0)
    top = lax.broadcasted_iota(I32, (height, devices), 1) % count_y * 2
    place = jnp.concatenate([(row == top + k).astype(F32) for k in (0, 1, -1)], 1)
    return f32_dot(place, jnp.concatenate(parts, 0))


def sweep_kernel(height, width, count_y, where_ref, gathered, adjacency, out_ref, links, gain_ref):
    grid = on_grid(gathered[...], height, count_y)
    links[...] = jnp.zeros_like(links)
    links[:, :, :width] = adjacency[...]
    row = lax.broadcasted_iota(I32, (height, LANES), 0)
    column = lax.broadcasted_iota(I32, (height, LANES), 1)
    below = (links[1] > 0) & (row < height - 1) & (column < width)
    beside = (links[0] > 0) & (column < width - 1)

    def lanes_of(k, present):
        values = grid if k == 0 else pltpu.roll(grid, LANES - 32 * k, 1)
        return jnp.where(present, values, 0.0)

    conf_down, off_down = lanes_of(0, below), lanes_of(1, below)
    conf_right, off_right = lanes_of(2, beside), lanes_of(3, beside)
    up = lambda a: pltpu.roll(a, 1, 0)
    down = lambda a: pltpu.roll(a, height - 1, 0)
    lefts = lambda a: pltpu.roll(a, 1, 1)
    rights = lambda a: pltpu.roll(a, LANES - 1, 1)
    conf_up, off_up = up(conf_down), -up(off_down)
    conf_left, off_left = lefts(conf_right), -lefts(off_right)
    scale = 1.0 / (anchor_weight + conf_up + conf_down + conf_left + conf_right)
    constant = scale * (
        conf_up * off_up + conf_down * off_down + conf_left * off_left + conf_right * off_right
    )
    a_up, a_down, a_left, a_right = (scale * a for a in (conf_up, conf_down, conf_left, conf_right))

    def sweep(_, gain):
        fresh = (
            (a_up * up(gain) + a_down * down(gain))
            + (a_left * lefts(gain) + a_right * rights(gain))
            + constant
        )
        return fresh - jnp.sum(fresh) / (height * width)

    gain = lax.fori_loop(0, ITERS, sweep, jnp.zeros((height, LANES), F32), unroll=True)
    gain_ref[...] = pltpu.roll(gain, LANES - where_ref[1] * COLS, 1)
    out_ref[...] = gain_ref[pl.ds(where_ref[0] * ROWS, ROWS), :COLS]


def sweeps(gathered, adjacency, where):
    height, width = adjacency.shape[1:]
    return pl.pallas_call(
        functools.partial(sweep_kernel, height, width, height // ROWS),
        in_specs=[
            pl.BlockSpec(memory_space=pltpu.SMEM),
            pl.BlockSpec(memory_space=pltpu.VMEM),
            pl.BlockSpec(memory_space=pltpu.VMEM),
        ],
        out_specs=pl.BlockSpec(memory_space=pltpu.VMEM),
        out_shape=jax.ShapeDtypeStruct((ROWS, COLS), F32),
        scratch_shapes=[pltpu.VMEM((2, height, LANES), I32), pltpu.VMEM((height, LANES), F32)],
    )(where, gathered, adjacency)


def body(pixels, weights, adjacency):
    px, w = by_lines(pixels), by_lines(weights)
    count_x, count_y = lax.axis_size("gx"), lax.axis_size("gy")
    ahead = lambda n: [(i, i + 1) for i in range(n - 1)]
    back = lambda n: [(i + 1, i) for i in range(n - 1)]
    below = lax.ppermute(packed(px, w, 0, 1, 0), "gy", back(count_y))
    above = lax.ppermute(packed(px, w, 6, 1, 1), "gy", ahead(count_y))
    left = lax.ppermute(packed(px, w, 3, 4, 3), "gx", ahead(count_x))
    inner = inner_sums(px, w)
    results = outer_results(px, w, below, above, left, inner, count_x * count_y)
    gathered = lax.all_to_all(results, ALL, 0, 0, tiled=True)
    where = jnp.stack([lax.axis_index("gy"), lax.axis_index("gx")]).astype(I32)
    return sweeps(gathered, adjacency, where)


def solution(mesh):
    return jax.shard_map(
        body,
        mesh=mesh,
        in_specs=(P("gy", "gx", None, None), P("gy", "gx", None, None), P()),
        out_specs=P("gy", "gx"),
        check_vma=False,
    )
```

profile of v0, /device:TPU:1, one launch (start us, length us, event | category | flops | bytes accessed | tf_op | source)
XLA Modules:
  0.0 111.5 jit_solution(6258548524845105216)
XLA Ops:
  0.0 6.3 %shard_map.55 = bf16[2,2,1024,128]{3,2,1,0:T(8,128)(2,1)} custom-call(s32[8,4096,128]{2,1,0:T(8,128)} %bitcast.16, bf16[8,4096,128]{2,1,0:T(8,128)(2,1)} %bitcast.22), custom_call_target="tpu_custom_call" | custom-call | flops 1048576 | bytes 7340032 | tf_op jit(solution)/shard_map/pallas_call | solution.py:45
  6.3 1.3 %collective-permute-start = (bf16[2,2,1024,128]{3,2,1,0:T(8,128)(2,1)}, bf16[2,2,1024,128]{3,2,1,0:T(8,128)(2,1)S(1)}, u32[]{:S(2)}, u32[]{:S(2)}) collective-permute-start(bf16[2,2,1024,128]{3,2,1,0:T(8,128)(2,1)} %shard_map.55), channel_id=1, source_target_pairs={{1,0},{2,1},{3,2},{4,3},{5,4},{6,5},{7,6},{8,7},{9,8},{10,9},{11,1... | collective-permute-start | bytes 3145736 | tf_op jit(solution)/shard_map/ppermute | solution.py:303
  7.6 6.4 %shard_map.56 = bf16[2,2,1024,128]{3,2,1,0:T(8,128)(2,1)} custom-call(s32[8,4096,128]{2,1,0:T(8,128)} %bitcast.17, bf16[8,4096,128]{2,1,0:T(8,128)(2,1)} %bitcast.23), custom_call_target="tpu_custom_call" | custom-call | flops 1048576 | bytes 7340032 | tf_op jit(solution)/shard_map/pallas_call | solution.py:45
  14.0 4.6 %collective-permute-start.1 = (bf16[2,2,1024,128]{3,2,1,0:T(8,128)(2,1)}, bf16[2,2,1024,128]{3,2,1,0:T(8,128)(2,1)S(1)}, u32[]{:S(2)}, u32[]{:S(2)}) collective-permute-start(bf16[2,2,1024,128]{3,2,1,0:T(8,128)(2,1)} %shard_map.56), channel_id=1, source_target_pairs={{0,1},{1,2},{2,3},{3,4},{4,5},{5,6},{6,7},{7,8},{8,9},{9,10},{10,1... | collective-permute-start | bytes 3145736 | tf_op jit(solution)/shard_map/ppermute | solution.py:304
  18.6 6.4 %shard_map.57 = bf16[2,2,1024,128]{3,2,1,0:T(8,128)(2,1)} custom-call(s32[8,4096,128]{2,1,0:T(8,128)} %bitcast.18, bf16[8,4096,128]{2,1,0:T(8,128)(2,1)} %bitcast.24), custom_call_target="tpu_custom_call" | custom-call | flops 1048576 | bytes 7340032 | tf_op jit(solution)/shard_map/pallas_call | solution.py:45
  25.0 4.6 %collective-permute-start.2 = (bf16[2,2,1024,128]{3,2,1,0:T(8,128)(2,1)}, bf16[2,2,1024,128]{3,2,1,0:T(8,128)(2,1)S(1)}, u32[]{:S(2)}, u32[]{:S(2)}) collective-permute-start(bf16[2,2,1024,128]{3,2,1,0:T(8,128)(2,1)} %shard_map.57), channel_id=1, source_target_pairs={{0,16},{16,32},{32,48},{48,64},{64,80},{80,96},{96,112},{1,17},{17... | collective-permute-start | bytes 3145736 | tf_op jit(solution)/shard_map/ppermute | solution.py:305
  29.5 30.5 %shard_map.58.inner = f32[10,2,16,256]{3,2,1,0:T(8,128)} custom-call(s32[10,4]{1,0:T(8,128)} %constant.13.clone.table, s32[8,4096,128]{2,1,0:T(8,128)} %bitcast.19, s32[8,4096,128]{2,1,0:T(8,128)} %bitcast.20, bf16[8,4096,128]{2,1,0:T(8,128)(2,1)} %bitcast.25, bf16[8,4096,128]{2,1,0:T(8,128)(2,1)} %bitcast.26), custom_call_target="tpu_custom_call" | custom-call | flops 21474836480 | bytes 62914560 | tf_op jit(solution)/shard_map/pallas_call | solution.py:102
  60.0 0.0 collective-permute-done.below
  60.0 0.0 copy-start.1
  60.0 0.0 collective-permute-done.1.above
  60.0 0.0 copy-start.2
  60.0 0.0 collective-permute-done.2.left
  60.0 0.9 copy-done.1
  61.0 0.4 copy-done.2
  61.3 0.0 copy-start.3
  61.3 1.0 copy-done.3
  62.4 21.1 %shard_map.59 = f32[128,128]{1,0:T(8,128)} custom-call(s32[6,2]{1,0:T(8,128)} %constant.14.clone.table, s32[8,4096,128]{2,1,0:T(8,128)} %bitcast.21, bf16[8,4096,128]{2,1,0:T(8,128)(2,1)} %bitcast.27, bf16[2,2,1024,128]{3,2,1,0:T(8,128)(2,1)} %copy-done.1, bf16[2,2,1024,128]{3,2,1,0:T(8,128)(2,1)} %copy-done.2, bf16[2,2,1024,128]{3,2,1,0:T(8,128)(2,1)} %copy-done.3, ...), custom_call_target="tpu_custom_call" | custom-call | flops 12884901888 | bytes 25165824 | tf_op jit(solution)/shard_map/pallas_call | solution.py:194
  83.4 11.4 %all-to-all-start = ((f32[128,1,128]{2,1,0:T(1,128)}), f32[128,1,128]{2,1,0:T(1,128)S(1)}, u32[]{:S(2)}, u32[]{:S(2)}) async-start(f32[128,1,128]{2,1,0:T(1,128)} %bitcast.29), calls=%async_computation | async-start | bytes 131072 | tf_op jit(solution)/shard_map/all_to_all | solution.py:308
  94.9 0.6 pad_add_fusion.where_ref
  95.5 9.2 %all-to-all-done = f32[128,1,128]{2,1,0:T(1,128)S(1)} async-done(((f32[128,1,128]{2,1,0:T(1,128)}), f32[128,1,128]{2,1,0:T(1,128)S(1)}, u32[]{:S(2)}, u32[]{:S(2)}) %all-to-all-start) | async-done | bytes 65568 | tf_op jit(solution)/shard_map/all_to_all | solution.py:308
  104.7 0.0 copy-start
  104.7 0.6 copy-done
  105.3 6.2 %shard_map.60 = f32[2,4]{1,0:T(2,128)} custom-call(s32[2]{0:T(128)} %pad_add_fusion.where_ref, f32[128,128]{1,0:T(8,128)} %bitcast.28, s32[2,32,32]{2,1,0:T(8,128)} %adjacency.1), custom_call_target="tpu_custom_call" | custom-call | tf_op jit(solution)/shard_map/pallas_call | solution.py:285
Async XLA Ops:
  6.3 53.7 %collective-permute-start = (bf16[2,2,1024,128]{3,2,1,0:T(8,128)(2,1)}, bf16[2,2,1024,128]{3,2,1,0:T(8,128)(2,1)S(1)}, u32[]{:S(2)}, u32[]{:S(2)}) collective-permute-start(bf16[2,2,1024,128]{3,2,1,0:T(8,128)(2,1)} %shard_map.55), channel_id=1, source_target_pairs={{1,0},{2,1},{3,2},{4,3},{5,4},{6,5},{7,6},{8,7},{9,8},{10,9},{11,1... | collective-permute-start | bytes 3145736 | tf_op jit(solution)/shard_map/ppermute | solution.py:303
  14.0 46.0 %collective-permute-start.1 = (bf16[2,2,1024,128]{3,2,1,0:T(8,128)(2,1)}, bf16[2,2,1024,128]{3,2,1,0:T(8,128)(2,1)S(1)}, u32[]{:S(2)}, u32[]{:S(2)}) collective-permute-start(bf16[2,2,1024,128]{3,2,1,0:T(8,128)(2,1)} %shard_map.56), channel_id=1, source_target_pairs={{0,1},{1,2},{2,3},{3,4},{4,5},{5,6},{6,7},{7,8},{8,9},{9,10},{10,1... | collective-permute-start | bytes 3145736 | tf_op jit(solution)/shard_map/ppermute | solution.py:304
  25.0 35.1 %collective-permute-start.2 = (bf16[2,2,1024,128]{3,2,1,0:T(8,128)(2,1)}, bf16[2,2,1024,128]{3,2,1,0:T(8,128)(2,1)S(1)}, u32[]{:S(2)}, u32[]{:S(2)}) collective-permute-start(bf16[2,2,1024,128]{3,2,1,0:T(8,128)(2,1)} %shard_map.57), channel_id=1, source_target_pairs={{0,16},{16,32},{32,48},{48,64},{64,80},{80,96},{96,112},{1,17},{17... | collective-permute-start | bytes 3145736 | tf_op jit(solution)/shard_map/ppermute | solution.py:305
  60.0 1.0 copy-start.1
  60.0 1.3 %copy-start.2 = (bf16[2,2,1024,128]{3,2,1,0:T(8,128)(2,1)}, bf16[2,2,1024,128]{3,2,1,0:T(8,128)(2,1)S(1)}, u32[]{:S(2)}) copy-start(bf16[2,2,1024,128]{3,2,1,0:T(8,128)(2,1)S(1)} %collective-permute-done.1.above) | copy-start | bytes 3145732
  61.3 1.0 copy-start.3
  83.4 21.2 %all-to-all-start = ((f32[128,1,128]{2,1,0:T(1,128)}), f32[128,1,128]{2,1,0:T(1,128)S(1)}, u32[]{:S(2)}, u32[]{:S(2)}) async-start(f32[128,1,128]{2,1,0:T(1,128)} %bitcast.29), calls=%async_computation | async-start | bytes 131072 | tf_op jit(solution)/shard_map/all_to_all | solution.py:308
  104.7 0.6 copy-start
where the time goes:
time: 112 us; the launch traced here: 111 us
  Pallas kernels  76.8 us (69%)
  starting transfers between devices  21.9 us (20%)
  waiting for transfers between devices  9.18 us (8%)
  local copies, waits for them, and re-layouts  2.97 us (3%)
    pallas_call x1, Pallas kernels, inner_sums(): pl.pallas_call(inner_kernel, grid_spec=pltpu.PrefetchScalarGridSpec(num_s...  30.5 us
    pallas_call x1, Pallas kernels, outer_results(): pl.pallas_call(outer_kernel, grid_spec=pltpu.PrefetchScalarGridSpec(num_s...  21.1 us
    pallas_call x3, Pallas kernels, packed(): pl.pallas_call(functools.partial(pack_kernel, side, lines), grid=(2, LINE...  19 us
    all_to_all x1, starting transfers between devices, body(): gathered = lax.all_to_all(results, ALL, 0, 0, tiled=True)  11.4 us
    all_to_all x1, waiting for transfers between devices, body(): gathered = lax.all_to_all(results, ALL, 0, 0, tiled=True)  9.17 us
    pallas_call x1, Pallas kernels, sweeps(): pl.pallas_call(functools.partial(sweep_kernel, height, width, height // R...  6.18 us
    ppermute x1, starting transfers between devices, body(): above = lax.ppermute(packed(px, w, 6, 1, 1), 'gy', ahead(count_y))  4.63 us
    ppermute x1, starting transfers between devices, body(): left = lax.ppermute(packed(px, w, 3, 4, 3), 'gx', ahead(count_x))  4.56 us
  transfers between devices with their start and end apart: 4, of which 1 were waited for; matrix products, arithmetic and copies ran while one was open for 1% of the time, Pallas kernels for 39%

commit v1 on v0

v1 whole, which is shorter than its diff:
```python
import functools

import jax
import jax.numpy as jnp
import numpy as np
from jax import lax
from jax.experimental import pallas as pl
from jax.experimental.pallas import tpu as pltpu
from jax.sharding import PartitionSpec as P

ITERS = 20
ROWS, COLS = 2, 4
CHUNKS, LANES = 1024, 128
LINES = 4 * CHUNKS
BATCH = 2
GROUP = 16
ALL = ("gx", "gy")
F32, BF16, I32 = jnp.float32, jnp.bfloat16, jnp.int32
VMEM_BYTES = 48 << 20

anchor_weight = 0.5
mismatch_scale = 8.0

INNER = np.array(
    [(c, 1, 4 + c, 0) for c in range(4)]
    + [(4 * r + c, 3, 4 * r + c + 1, 2) for r in range(2) for c in range(3)],
    np.int32,
)
SENT = (((0, 0), (1, 0)), ((6, 1), (7, 1)), ((3, 3), (7, 3)))
OUTER = np.array([(4, 1), (5, 1), (2, 0), (3, 0), (0, 2), (4, 2)], np.int32)


def pack_kernel(px, w, below_ref, above_ref, left_ref, pixels, tiles, wide, px_arrived, w_arrived):
    jobs = [(out, n) + SENT[k][n] for k, out in enumerate((below_ref, above_ref, left_ref)) for n in range(2)]
    needed = sorted({job[2] for job in jobs}, key=[job[2] for job in jobs].index)
    w_copies = [
        pltpu.make_async_copy(w.at[tile], tiles.at[k], w_arrived.at[k]) for k, tile in enumerate(needed)
    ]
    px_copies = [
        pltpu.make_async_copy(px.at[job[2], :, job[3], :], pixels.at[k], px_arrived.at[k])
        for k, job in enumerate(jobs)
    ]
    for copy in w_copies + px_copies:
        copy.start()
    for k, tile in enumerate(needed):
        w_copies[k].wait()
        wide[k % 2] = tiles[k].astype(F32)
        for out, n, _, side in (job for job in jobs if job[2] == tile):
            out[n, 1] = wide[k % 2, pl.ds(side, CHUNKS, stride=4), :].astype(BF16)
    for k, (out, n, _, _) in enumerate(jobs):
        px_copies[k].wait()
        out[n, 0] = pixels[k].astype(F32).astype(BF16)


def packed(px, w):
    strips = jax.ShapeDtypeStruct((2, 2, CHUNKS, LANES), BF16)
    vmem = pl.BlockSpec(memory_space=pltpu.VMEM)
    return pl.pallas_call(
        pack_kernel,
        in_specs=[pl.BlockSpec(memory_space=pl.ANY)] * 2,
        out_specs=[vmem] * 3,
        out_shape=[strips] * 3,
        scratch_shapes=[
            pltpu.VMEM((6, CHUNKS, LANES), I32),
            pltpu.VMEM((5, LINES, LANES), BF16),
            pltpu.VMEM((2, LINES, LANES), F32),
            pltpu.SemaphoreType.DMA((6,)),
            pltpu.SemaphoreType.DMA((5,)),
        ],
        compiler_params=pltpu.CompilerParams(vmem_limit_bytes=VMEM_BYTES),
        cost_estimate=pl.CostEstimate(flops=1 << 20, bytes_accessed=8 << 20, transcendentals=0),
    )(px, w)


def one_hot_pair(bins, joint):
    upper = lax.shift_right_logical(bins, 4).astype(F32).astype(BF16)
    lower = (bins & 15).astype(F32).astype(BF16)
    zero, one = jnp.zeros((), BF16), jnp.ones((), BF16)
    left = [jnp.where(upper == BF16(k), joint, zero) for k in range(16)]
    right = [jnp.where(lower == BF16(k), one, zero) for k in range(16)]
    return jnp.concatenate(left, 0), jnp.concatenate(right, 0)


def diagonal_sum(product):
    column = lax.broadcasted_iota(I32, (GROUP, 256), 1) % GROUP
    row = lax.broadcasted_iota(I32, (GROUP, 256), 0)
    kept = jnp.where((column == row)[None], product.reshape(16, GROUP, 256), 0.0)
    return jnp.sum(kept, axis=1)


def strip_products(sums, strips):
    for part in range(CHUNKS // GROUP // 2):
        pairs = zip(*(strips(2 * part + half) for half in range(2)))
        for unit, halves in enumerate(pairs):
            left, right = zip(*(one_hot_pair(bins, joint) for bins, joint in halves))
            pltpu.matmul_push_rhs(jnp.concatenate(right, 1), part % 2, unit, transpose=True)
            pltpu.matmul_acc_lhs(sums[unit], jnp.concatenate(left, 1), load_staged_rhs=part % 2)


def with_sums(function):
    units = [pltpu.ACC(unit)((256, 256), F32) for _ in range(BATCH) for unit in range(2)]
    pl.run_scoped(lambda *refs: function([refs[:2], refs[2:]]), *units)


def entry(table, step, column):
    values = [int(v) for v in table[:, column]]
    chosen = jnp.int32(values[0])
    for k in range(1, len(values)):
        if values[k] != values[k - 1]:
            chosen = jnp.where(step >= k, jnp.int32(values[k]), chosen)
    return chosen


def fetch(px, w, table, step, buffers, tiles, arrived, slot, item):
    tile, side = entry(table, step, 2 * item), entry(table, step, 2 * item + 1)
    return (
        pltpu.make_async_copy(px.at[tile, :, side, :], buffers.at[slot, item], arrived.at[slot, item, 0]),
        pltpu.make_async_copy(w.at[tile], tiles.at[slot, item], arrived.at[slot, item, 1]),
    )


def start_next(items, *refs):
    n, steps = pl.program_id(0), pl.num_programs(0)
    px, w, table, buffers, tiles, arrived = refs
    slot = lax.rem(n, 2)

    def start(step, place):
        for item in range(items):
            for copy in fetch(px, w, table, step, buffers, tiles, arrived, place, item):
                copy.start()

    @pl.when(n == 0)
    def _():
        start(0, 0)

    @pl.when(n + 1 < steps)
    def _():
        start(n + 1, 1 - slot)

    return slot


def side_of(tiles, wide, slot, item, side, v):
    o = 4 * GROUP * v
    wide[item, o : o + 4 * GROUP] = tiles[slot, item, o : o + 4 * GROUP].astype(F32)
    return wide[item, pl.ds(o + side, GROUP, stride=4), :]


def inner_kernel(table, px, w, out_ref, buffers, tiles, wide, arrived):
    n = pl.program_id(0)
    slot = start_next(2 * BATCH, px, w, table, buffers, tiles, arrived)

    def steps(sums):
        def finish(pair):
            for place in range(2):
                rows = slice(16 * pair, 16 * pair + 16)
                out_ref[place, rows] = diagonal_sum(pltpu.matmul_pop(sums[pair][place]))

        for pair in range(BATCH):
            items = (2 * pair, 2 * pair + 1)
            for item in items:
                for copy in fetch(px, w, table, n, buffers, tiles, arrived, slot, item):
                    copy.wait()

            def strips(v):
                weight_a, weight_b = (
                    side_of(tiles, wide, slot, item, entry(table, n, 2 * item + 1), v) for item in items
                )
                joint = (weight_a * weight_b).astype(BF16)
                dense = slice(GROUP * v, GROUP * (v + 1))
                return [(buffers[slot, item, dense], joint) for item in items]

            strip_products(sums[pair], strips)
            if pair > 0:
                finish(pair - 1)
        finish(BATCH - 1)

    with_sums(steps)


def inner_sums(px, w):
    steps = len(INNER) // BATCH
    return pl.pallas_call(
        functools.partial(inner_kernel, INNER.reshape(steps, 4 * BATCH)),
        grid=(steps,),
        in_specs=[pl.BlockSpec(memory_space=pl.ANY)] * 2,
        out_specs=pl.BlockSpec((2, BATCH * 16, 256), lambda n: (0, n, 0)),
        scratch_shapes=[
            pltpu.VMEM((2, 2 * BATCH, CHUNKS, LANES), I32),
            pltpu.VMEM((2, 2 * BATCH, LINES, LANES), BF16),
            pltpu.VMEM((2 * BATCH, LINES, LANES), F32),
            pltpu.SemaphoreType.DMA((2, 2 * BATCH, 2)),
        ],
        out_shape=jax.ShapeDtypeStruct((2, len(INNER) * 16, 256), F32),
        compiler_params=pltpu.CompilerParams(vmem_limit_bytes=VMEM_BYTES),
        cost_estimate=pl.CostEstimate(
            flops=len(INNER) * 4 * 256 * 256 * 8192, bytes_accessed=30 << 20, transcendentals=0
        ),
    )(px, w)


def outer_kernel(
    table, px, w, below, above, left, out_ref, buffers, tiles, wide, arrived
):
    n = pl.program_id(0)
    slot = start_next(BATCH, px, w, table, buffers, tiles, arrived)

    def steps(sums):
        def finish(pair):
            own, other = (diagonal_sum(pltpu.matmul_pop(sums[pair][place])) for place in range(2))
            rows = slice(16 * pair, 16 * pair + 16)
            out_ref[0, rows] = jnp.where(n == 0, own, other)
            out_ref[1, rows] = jnp.where(n == 0, other, own)

        for pair in range(BATCH):
            for copy in fetch(px, w, table, n, buffers, tiles, arrived, slot, pair):
                copy.wait()

            def strips(v):
                dense = slice(GROUP * v, GROUP * (v + 1))

                def far(k):
                    return jnp.where(
                        n == 0, below[pair, k, dense],
                        jnp.where(n == 1, above[pair, k, dense], left[pair, k, dense]),
                    ).astype(F32)

                own = side_of(tiles, wide, slot, pair, entry(table, n, 2 * pair + 1), v)
                joint = (own * far(1)).astype(BF16)
                return (buffers[slot, pair, dense], joint), (far(0).astype(I32), joint)

            strip_products(sums[pair], strips)
            if pair > 0:
                finish(pair - 1)
        finish(BATCH - 1)

    with_sums(steps)


def outer_sums(px, w, below, above, left):
    count = len(OUTER)
    vmem = pl.BlockSpec(memory_space=pltpu.VMEM)
    return pl.pallas_call(
        functools.partial(outer_kernel, OUTER.reshape(count // BATCH, 2 * BATCH)),
        grid=(count // BATCH,),
        in_specs=[pl.BlockSpec(memory_space=pl.ANY)] * 2 + [vmem] * 3,
        out_specs=pl.BlockSpec((2, BATCH * 16, 256), lambda n: (0, n, 0)),
        scratch_shapes=[
            pltpu.VMEM((2, BATCH, CHUNKS, LANES), I32),
            pltpu.VMEM((2, BATCH, LINES, LANES), BF16),
            pltpu.VMEM((BATCH, LINES, LANES), F32),
            pltpu.SemaphoreType.DMA((2, BATCH, 2)),
        ],
        out_shape=jax.ShapeDtypeStruct((2, count * 16, 256), F32),
        compiler_params=pltpu.CompilerParams(vmem_limit_bytes=VMEM_BYTES),
        cost_estimate=pl.CostEstimate(
            flops=count * 4 * 256 * 256 * 8192, bytes_accessed=9 << 20, transcendentals=0
        ),
    )(px, w, below, above, left)


def pieces(x):
    high = x.astype(BF16)
    rest = x - high.astype(F32)
    middle = rest.astype(BF16)
    return high, middle, (rest - middle.astype(F32)).astype(BF16)


def apply(coefficients, x):
    exact = coefficients.astype(BF16)
    return jnp.dot(
        jnp.concatenate([exact] * 3, 1), jnp.concatenate(pieces(x), 0), preferred_element_type=F32
    )


def apply_right(x, coefficients):
    exact = coefficients.astype(BF16)
    return jnp.dot(
        jnp.concatenate(pieces(x), 1), jnp.concatenate([exact] * 3, 0), preferred_element_type=F32
    )


def pair_results(first, second):
    iota = lambda shape, dim: lax.broadcasted_iota(I32, shape, dim)
    difference = first - second
    within = (iota((256, LANES), 0) // GROUP <= iota((256, LANES), 1)) & (iota((256, LANES), 1) < 16)
    row, other = iota((256, 256), 0), iota((256, 256), 1)
    before = (row // 16 == other // 16) & (other < row)
    earlier = jnp.sum(apply(before.astype(F32), difference), axis=1, keepdims=True)
    cumulative = apply_right(difference, within.astype(F32)) + earlier
    size = jnp.where(iota((256, LANES), 1) < 16, jnp.abs(cumulative), 0.0)
    pair, member = iota((32, 256), 0), iota((32, 256), 1)
    mine = pair % 16 == member // 16
    heights = jnp.where(mine, jnp.where(pair < 16, 1, member % 16 * 16), 0).astype(F32)
    sums = apply(heights, jnp.concatenate([first, second, size], 1))
    lower = (iota((16, 256), 1) // GROUP).astype(F32) + 0.5
    reduce = lambda x: jnp.sum(x, axis=1, keepdims=True)
    total = reduce(sums[:16, :256])
    mean_first = reduce(sums[:16, :256] * lower + sums[16:, :256]) / total
    mean_second = reduce(sums[:16, 256:512] * lower + sums[16:, 256:512]) / total
    distance = reduce(sums[:16, 512:]) / total
    mismatch = (distance - jnp.abs(mean_first - mean_second)) / mismatch_scale
    confidence = 1.0 / (0.25 + mismatch * mismatch)
    offset = jnp.log(mean_second) - jnp.log(mean_first)
    number, lane = iota((16, LANES), 0), iota((16, LANES), 1)
    spread = jnp.where(number == lane, confidence, jnp.where(number == lane - 16, offset, 0.0))
    return jnp.sum(jnp.where(total > 0, spread, 0.0), axis=0, keepdims=True)


def results_kernel(inner, outer, out_ref):
    first, second = (jnp.concatenate([inner[k], outer[k]], 0) for k in range(2))
    out_ref[...] = jnp.broadcast_to(pair_results(first, second), out_ref.shape)


def results(inner, outer, devices):
    return pl.pallas_call(
        results_kernel,
        in_specs=[pl.BlockSpec(memory_space=pltpu.VMEM)] * 2,
        out_specs=pl.BlockSpec(memory_space=pltpu.VMEM),
        out_shape=jax.ShapeDtypeStruct((devices, LANES), F32),
    )(inner, outer)


def on_grid(gathered, height, count_y):
    devices = gathered.shape[0]
    slot = lax.broadcasted_iota(I32, (LANES, LANES), 0)
    lane = lax.broadcasted_iota(I32, (LANES, LANES), 1)
    c, odd, right = lane % 4, lane // 32 % 2, lane // 64 == 1
    offset_slots = 16 * odd
    edge = right & (c == 3)
    slots = [
        jnp.where(edge, 14, jnp.where(right, 4 + c, c)),
        jnp.where(edge, 15, jnp.where(right, 7 + c, jnp.where(c < 2, 10 + c, -100))),
        jnp.where(right | (c < 2), -100, 10 + c),
    ]
    choose = jnp.concatenate([(slot == s + offset_slots).astype(F32) for s in slots], 1)
    chosen = apply_right(gathered, choose)
    device = lax.broadcasted_iota(I32, (devices, LANES), 0)
    lane = lax.broadcasted_iota(I32, (devices, LANES), 1)
    shifted = ((lane // 64 == 1) & (lane % 4 == 3)).astype(I32)
    here = device // count_y == lane % 32 // 4 + shifted
    parts = [jnp.where(here, chosen[:, LANES * k : LANES * (k + 1)], 0.0) for k in range(3)]
    row = lax.broadcasted_iota(I32, (height, devices), 0)
    top = lax.broadcasted_iota(I32, (height, devices), 1) % count_y * 2
    place = jnp.concatenate([(row == top + k).astype(F32) for k in (0, 1, -1)], 1)
    return apply(place, jnp.concatenate(parts, 0))


def sweep_kernel(height, width, count_y, where_ref, gathered, adjacency, out_ref, links, gain_ref):
    grid = on_grid(gathered[...], height, count_y)
    links[...] = jnp.zeros_like(links)
    links[:, :, :width] = adjacency[...]
    row = lax.broadcasted_iota(I32, (height, LANES), 0)
    column = lax.broadcasted_iota(I32, (height, LANES), 1)
    below = (links[1] > 0) & (row < height - 1) & (column < width)
    beside = (links[0] > 0) & (column < width - 1)

    def lanes_of(k, present):
        values = grid if k == 0 else pltpu.roll(grid, LANES - 32 * k, 1)
        return jnp.where(present, values, 0.0)

    conf_down, off_down = lanes_of(0, below), lanes_of(1, below)
    conf_right, off_right = lanes_of(2, beside), lanes_of(3, beside)
    up = lambda a: pltpu.roll(a, 1, 0)
    down = lambda a: pltpu.roll(a, height - 1, 0)
    lefts = lambda a: pltpu.roll(a, 1, 1)
    rights = lambda a: pltpu.roll(a, LANES - 1, 1)
    conf_up, off_up = up(conf_down), -up(off_down)
    conf_left, off_left = lefts(conf_right), -lefts(off_right)
    scale = 1.0 / (anchor_weight + conf_up + conf_down + conf_left + conf_right)
    constant = scale * (
        conf_up * off_up + conf_down * off_down + conf_left * off_left + conf_right * off_right
    )
    a_up, a_down, a_left, a_right = (scale * a for a in (conf_up, conf_down, conf_left, conf_right))

    ones = a_up + a_down + a_left + a_right

    def mean(a):
        columns = jnp.sum(a, axis=0, keepdims=True)
        return jnp.sum(columns, axis=1, keepdims=True) * (1.0 / (height * width))

    def sweep(_, fresh):
        spread = (
            (a_up * up(fresh) + a_down * down(fresh))
            + (a_left * lefts(fresh) + a_right * rights(fresh))
            + constant
        )
        return spread - mean(fresh) * ones

    fresh = lax.fori_loop(0, ITERS - 1, sweep, constant, unroll=True)
    gain = fresh - mean(fresh)
    gain_ref[...] = pltpu.roll(gain, LANES - where_ref[1] * COLS, 1)
    out_ref[...] = gain_ref[pl.ds(where_ref[0] * ROWS, ROWS), :COLS]


def sweeps(gathered, adjacency, where):
    height, width = adjacency.shape[1:]
    return pl.pallas_call(
        functools.partial(sweep_kernel, height, width, height // ROWS),
        in_specs=[
            pl.BlockSpec(memory_space=pltpu.SMEM),
            pl.BlockSpec(memory_space=pltpu.VMEM),
            pl.BlockSpec(memory_space=pltpu.VMEM),
        ],
        out_specs=pl.BlockSpec(memory_space=pltpu.VMEM),
        out_shape=jax.ShapeDtypeStruct((ROWS, COLS), F32),
        scratch_shapes=[pltpu.VMEM((2, height, LANES), I32), pltpu.VMEM((height, LANES), F32)],
    )(where, gathered, adjacency)


def body(pixels, weights, adjacency):
    px = pixels.reshape(ROWS * COLS, 4, CHUNKS, LANES).transpose(0, 2, 1, 3)
    w = weights.reshape(ROWS * COLS, 4, CHUNKS, LANES).transpose(0, 2, 1, 3)
    w = w.reshape(ROWS * COLS, LINES, LANES)
    count_x, count_y = lax.axis_size("gx"), lax.axis_size("gy")
    ahead = lambda n: [(i, i + 1) for i in range(n - 1)]
    back = lambda n: [(i + 1, i) for i in range(n - 1)]
    below, above, left = packed(px, w)
    below = lax.ppermute(below, "gy", back(count_y))
    above = lax.ppermute(above, "gy", ahead(count_y))
    left = lax.ppermute(left, "gx", ahead(count_x))
    inner = inner_sums(px, w)
    outer = outer_sums(px, w, below, above, left)
    gathered = lax.all_to_all(results(inner, outer, count_x * count_y), ALL, 0, 0, tiled=True)
    where = jnp.stack([lax.axis_index("gy"), lax.axis_index("gx")]).astype(I32)
    return sweeps(gathered, adjacency, where)


def solution(mesh):
    return jax.shard_map(
        body,
        mesh=mesh,
        in_specs=(P("gy", "gx", None, None), P("gy", "gx", None, None), P()),
        out_specs=P("gy", "gx"),
        check_vma=False,
    )
```

time: 112 us -> 88.3 us (0.79)
  Pallas kernels: 76.8 us -> 54.2 us
    pallas_call x5 -> x4, Pallas kernels: 70.6 us -> 50.4 us  [the longest x1 26 us: inner_sums(): pl.pallas_call(functools.partial(inner_kernel, INNER.reshape(steps, 4 * B...]
    pallas_call x1, Pallas kernels: 6.18 us -> 3.85 us  [sweeps(): pl.pallas_call(functools.partial(sweep_kernel, height, width, height // R...]
    unnamed x8 -> x6, local copies, waits for them, and re-layouts: 2.97 us -> 2.01 us
  transfers between devices with their start and end apart: 4 -> 4, of which waited for: 1 -> 1; matrix products, arithmetic and copies ran while one was open for 1% -> 1% of each run, Pallas kernels for 39% -> 29%
where the time goes in v1:
time: 88.3 us; the launch traced here: 88 us
  Pallas kernels  54.2 us (61%)
  starting transfers between devices  21.9 us (25%)
  waiting for transfers between devices  9.16 us (10%)
  local copies, waits for them, and re-layouts  2.01 us (2%)
    pallas_call x1, Pallas kernels, inner_sums(): pl.pallas_call(functools.partial(inner_kernel, INNER.reshape(steps, 4 * B...  26 us
    pallas_call x1, Pallas kernels, outer_sums(): pl.pallas_call(functools.partial(outer_kernel, OUTER.reshape(count // BAT...  17.1 us
    all_to_all x1, starting transfers between devices, body(): lax.all_to_all(results(inner, outer, count_x * count_y), ALL, 0, 0, tiled...  11.4 us
    all_to_all x1, waiting for transfers between devices, body(): lax.all_to_all(results(inner, outer, count_x * count_y), ALL, 0, 0, tiled...  9.15 us
    pallas_call x1, Pallas kernels, packed(): pl.pallas_call(pack_kernel, in_specs=[pl.BlockSpec(memory_space=pl.ANY)]...  5.04 us
    ppermute x1, starting transfers between devices, body(): above = lax.ppermute(above, 'gy', ahead(count_y))  4.64 us
    ppermute x1, starting transfers between devices, body(): left = lax.ppermute(left, 'gx', ahead(count_x))  4.57 us
    pallas_call x1, Pallas kernels, sweeps(): pl.pallas_call(functools.partial(sweep_kernel, height, width, height // R...  3.85 us
  transfers between devices with their start and end apart: 4, of which 1 were waited for; matrix products, arithmetic and copies ran while one was open for 1% of the time, Pallas kernels for 29%

profile of v1, /device:TPU:1, one launch (start us, length us, event | category | flops | bytes accessed | tf_op | source)
XLA Modules:
  0.0 88.0 jit_solution(6097015539567076724)
XLA Ops:
  0.0 5.0 %shard_map.38 = (bf16[2,2,1024,128]{3,2,1,0:T(8,128)(2,1)}, bf16[2,2,1024,128]{3,2,1,0:T(8,128)(2,1)}, bf16[2,2,1024,128]{3,2,1,0:T(8,128)(2,1)S(1)}) custom-call(s32[8,1024,4,128]{3,2,1,0:T(4,128)} %bitcast.14, bf16[8,4096,128]{2,1,0:T(8,128)(2,1)} %bitcast.17), custom_call_target="tpu_custom_call" | custom-call | flops 1048576 | bytes 8388608 | tf_op jit(solution)/shard_map/pallas_call | solution.py:58
  5.0 1.3 %collective-permute-start = (bf16[2,2,1024,128]{3,2,1,0:T(8,128)(2,1)}, bf16[2,2,1024,128]{3,2,1,0:T(8,128)(2,1)S(1)}, u32[]{:S(2)}, u32[]{:S(2)}) collective-permute-start(bf16[2,2,1024,128]{3,2,1,0:T(8,128)(2,1)} %get-tuple-element.8), channel_id=1, source_target_pairs={{1,0},{2,1},{3,2},{4,3},{5,4},{6,5},{7,6},{8,7},{9,8},{10,9},{11,1... | collective-permute-start | bytes 3145736 | tf_op jit(solution)/shard_map/ppermute | solution.py:419
  6.3 4.6 %collective-permute-start.1 = (bf16[2,2,1024,128]{3,2,1,0:T(8,128)(2,1)}, bf16[2,2,1024,128]{3,2,1,0:T(8,128)(2,1)S(1)}, u32[]{:S(2)}, u32[]{:S(2)}) collective-permute-start(bf16[2,2,1024,128]{3,2,1,0:T(8,128)(2,1)} %get-tuple-element.9), channel_id=1, source_target_pairs={{0,1},{1,2},{2,3},{3,4},{4,5},{5,6},{6,7},{7,8},{8,9},{9,10},{10,1... | collective-permute-start | bytes 3145736 | tf_op jit(solution)/shard_map/ppermute | solution.py:420
  11.0 4.6 %collective-permute-start.2 = (bf16[2,2,1024,128]{3,2,1,0:T(8,128)(2,1)S(1)}, bf16[2,2,1024,128]{3,2,1,0:T(8,128)(2,1)}, u32[]{:S(2)}, u32[]{:S(2)}) collective-permute-start(bf16[2,2,1024,128]{3,2,1,0:T(8,128)(2,1)S(1)} %get-tuple-element.10), channel_id=1, source_target_pairs={{0,16},{16,32},{32,48},{48,64},{64,80},{80,96},{96,112},{1,17},{17... | collective-permute-start | bytes 3145736 | tf_op jit(solution)/shard_map/ppermute | solution.py:421
  15.6 26.0 %shard_map.37.inner = f32[2,160,256]{2,1,0:T(8,128)S(1)} custom-call(s32[8,1024,4,128]{3,2,1,0:T(4,128)} %bitcast.15, bf16[8,4096,128]{2,1,0:T(8,128)(2,1)} %bitcast.18), custom_call_target="tpu_custom_call" | custom-call | flops 21474836480 | bytes 31457280 | tf_op jit(solution)/shard_map/pallas_call | solution.py:183
  41.5 0.0 copy-start
  41.5 0.7 copy-done
  42.3 0.0 collective-permute-done.below
  42.3 0.0 collective-permute-done.1.above
  42.3 0.0 collective-permute-done.2.left
  42.3 17.1 %shard_map.39.outer = f32[2,96,256]{2,1,0:T(8,128)S(1)} custom-call(s32[8,1024,4,128]{3,2,1,0:T(4,128)} %bitcast.16, bf16[8,4096,128]{2,1,0:T(8,128)(2,1)} %bitcast.19, bf16[2,2,1024,128]{3,2,1,0:T(8,128)(2,1)S(1)} %collective-permute-done.below, bf16[2,2,1024,128]{3,2,1,0:T(8,128)(2,1)S(1)} %collective-permute-done.1.above, ...), custom_call_target="tpu_custom_call" | custom-call | flops 12884901888 | bytes 9437184 | tf_op jit(solution)/shard_map/pallas_call | solution.py:243
  59.3 0.0 copy-start.1
  59.3 0.7 copy-done.1
  60.0 2.3 %shard_map.40 = f32[128,128]{1,0:T(8,128)} custom-call(f32[2,160,256]{2,1,0:T(8,128)} %copy-done, f32[2,96,256]{2,1,0:T(8,128)} %copy-done.1), custom_call_target="tpu_custom_call" | custom-call | tf_op jit(solution)/shard_map/pallas_call | solution.py:316
  62.4 11.4 %all-to-all-start = ((f32[128,1,128]{2,1,0:T(1,128)}), f32[128,1,128]{2,1,0:T(1,128)S(1)}, u32[]{:S(2)}, u32[]{:S(2)}) async-start(f32[128,1,128]{2,1,0:T(1,128)} %bitcast.20), calls=%async_computation | async-start | bytes 131072 | tf_op jit(solution)/shard_map/all_to_all | solution.py:424
  73.8 0.6 pad_add_fusion.where_ref
  74.4 9.2 %all-to-all-done = f32[128,1,128]{2,1,0:T(1,128)S(1)} async-done(((f32[128,1,128]{2,1,0:T(1,128)}), f32[128,1,128]{2,1,0:T(1,128)S(1)}, u32[]{:S(2)}, u32[]{:S(2)}) %all-to-all-start) | async-done | bytes 65568 | tf_op jit(solution)/shard_map/all_to_all | solution.py:424
  83.5 0.0 copy-start.2
  83.5 0.6 copy-done.2
  84.2 3.9 %shard_map.41 = f32[2,4]{1,0:T(2,128)} custom-call(s32[2]{0:T(128)} %pad_add_fusion.where_ref, f32[128,128]{1,0:T(8,128)} %bitcast.21, s32[2,32,32]{2,1,0:T(8,128)} %adjacency.1), custom_call_target="tpu_custom_call" | custom-call | tf_op jit(solution)/shard_map/pallas_call | solution.py:398
Async XLA Ops:
  5.0 37.2 %collective-permute-start = (bf16[2,2,1024,128]{3,2,1,0:T(8,128)(2,1)}, bf16[2,2,1024,128]{3,2,1,0:T(8,128)(2,1)S(1)}, u32[]{:S(2)}, u32[]{:S(2)}) collective-permute-start(bf16[2,2,1024,128]{3,2,1,0:T(8,128)(2,1)} %get-tuple-element.8), channel_id=1, source_target_pairs={{1,0},{2,1},{3,2},{4,3},{5,4},{6,5},{7,6},{8,7},{9,8},{10,9},{11,1... | collective-permute-start | bytes 3145736 | tf_op jit(solution)/shard_map/ppermute | solution.py:419
  6.3 35.9 %collective-permute-start.1 = (bf16[2,2,1024,128]{3,2,1,0:T(8,128)(2,1)}, bf16[2,2,1024,128]{3,2,1,0:T(8,128)(2,1)S(1)}, u32[]{:S(2)}, u32[]{:S(2)}) collective-permute-start(bf16[2,2,1024,128]{3,2,1,0:T(8,128)(2,1)} %get-tuple-element.9), channel_id=1, source_target_pairs={{0,1},{1,2},{2,3},{3,4},{4,5},{5,6},{6,7},{7,8},{8,9},{9,10},{10,1... | collective-permute-start | bytes 3145736 | tf_op jit(solution)/shard_map/ppermute | solution.py:420
  11.0 31.3 %collective-permute-start.2 = (bf16[2,2,1024,128]{3,2,1,0:T(8,128)(2,1)S(1)}, bf16[2,2,1024,128]{3,2,1,0:T(8,128)(2,1)}, u32[]{:S(2)}, u32[]{:S(2)}) collective-permute-start(bf16[2,2,1024,128]{3,2,1,0:T(8,128)(2,1)S(1)} %get-tuple-element.10), channel_id=1, source_target_pairs={{0,16},{16,32},{32,48},{48,64},{64,80},{80,96},{96,112},{1,17},{17... | collective-permute-start | bytes 3145736 | tf_op jit(solution)/shard_map/ppermute | solution.py:421
  41.5 0.7 copy-start
  59.3 0.7 copy-start.1
  62.4 21.2 %all-to-all-start = ((f32[128,1,128]{2,1,0:T(1,128)}), f32[128,1,128]{2,1,0:T(1,128)S(1)}, u32[]{:S(2)}, u32[]{:S(2)}) async-start(f32[128,1,128]{2,1,0:T(1,128)} %bitcast.20), calls=%async_computation | async-start | bytes 131072 | tf_op jit(solution)/shard_map/all_to_all | solution.py:424
  83.5 0.6 copy-start.2

commit v2 on v1

--- a/solution.py
+++ b/solution.py
@@ -12,11 +12,11 @@
 ROWS, COLS = 2, 4
 CHUNKS, LANES = 1024, 128
 LINES = 4 * CHUNKS
-BATCH = 2
+BATCH = 3
+OUTER_BATCH = 2
 GROUP = 16
 ALL = ("gx", "gy")
 F32, BF16, I32 = jnp.float32, jnp.bfloat16, jnp.int32
-VMEM_BYTES = 48 << 20
 
 anchor_weight = 0.5
 mismatch_scale = 8.0
@@ -30,48 +30,6 @@
 OUTER = np.array([(4, 1), (5, 1), (2, 0), (3, 0), (0, 2), (4, 2)], np.int32)
 
 
-def pack_kernel(px, w, below_ref, above_ref, left_ref, pixels, tiles, wide, px_arrived, w_arrived):
-    jobs = [(out, n) + SENT[k][n] for k, out in enumerate((below_ref, above_ref, left_ref)) for n in range(2)]
-    needed = sorted({job[2] for job in jobs}, key=[job[2] for job in jobs].index)
-    w_copies = [
-        pltpu.make_async_copy(w.at[tile], tiles.at[k], w_arrived.at[k]) for k, tile in enumerate(needed)
-    ]
-    px_copies = [
-        pltpu.make_async_copy(px.at[job[2], :, job[3], :], pixels.at[k], px_arrived.at[k])
-        for k, job in enumerate(jobs)
-    ]
-    for copy in w_copies + px_copies:
-        copy.start()
-    for k, tile in enumerate(needed):
-        w_copies[k].wait()
-        wide[k % 2] = tiles[k].astype(F32)
-        for out, n, _, side in (job for job in jobs if job[2] == tile):
-            out[n, 1] = wide[k % 2, pl.ds(side, CHUNKS, stride=4), :].astype(BF16)
-    for k, (out, n, _, _) in enumerate(jobs):
-        px_copies[k].wait()
-        out[n, 0] = pixels[k].astype(F32).astype(BF16)
-
-
-def packed(px, w):
-    strips = jax.ShapeDtypeStruct((2, 2, CHUNKS, LANES), BF16)
-    vmem = pl.BlockSpec(memory_space=pltpu.VMEM)
-    return pl.pallas_call(
-        pack_kernel,
-        in_specs=[pl.BlockSpec(memory_space=pl.ANY)] * 2,
-        out_specs=[vmem] * 3,
-        out_shape=[strips] * 3,
-        scratch_shapes=[
-            pltpu.VMEM((6, CHUNKS, LANES), I32),
-            pltpu.VMEM((5, LINES, LANES), BF16),
-            pltpu.VMEM((2, LINES, LANES), F32),
-            pltpu.SemaphoreType.DMA((6,)),
-            pltpu.SemaphoreType.DMA((5,)),
-        ],
-        compiler_params=pltpu.CompilerParams(vmem_limit_bytes=VMEM_BYTES),
-        cost_estimate=pl.CostEstimate(flops=1 << 20, bytes_accessed=8 << 20, transcendentals=0),
-    )(px, w)
-
-
 def one_hot_pair(bins, joint):
     upper = lax.shift_right_logical(bins, 4).astype(F32).astype(BF16)
     lower = (bins & 15).astype(F32).astype(BF16)
@@ -98,7 +56,7 @@
 
 
 def with_sums(function):
-    units = [pltpu.ACC(unit)((256, 256), F32) for _ in range(BATCH) for unit in range(2)]
+    units = [pltpu.ACC(unit)((256, 256), F32) for _ in range(2) for unit in range(2)]
     pl.run_scoped(lambda *refs: function([refs[:2], refs[2:]]), *units)
 
 
@@ -140,10 +98,75 @@
     return slot
 
 
-def side_of(tiles, wide, slot, item, side, v):
+def side_of(tiles, wide, place, room, side, v):
     o = 4 * GROUP * v
-    wide[item, o : o + 4 * GROUP] = tiles[slot, item, o : o + 4 * GROUP].astype(F32)
-    return wide[item, pl.ds(o + side, GROUP, stride=4), :]
+    wide[room, o : o + 4 * GROUP] = tiles[place, o : o + 4 * GROUP].astype(F32)
+    return wide[room, pl.ds(o + side, GROUP, stride=4), :]
+
+
+def pack_kernel(
+    px, w, below_ref, above_ref, left_ref, sums_ref, pixels, tiles, wide, px_arrived, w_arrived
+):
+    jobs = [(out, n) + SENT[k][n] for k, out in enumerate((below_ref, above_ref, left_ref)) for n in range(2)]
+    first = [tuple(int(v) for v in INNER[0, 2 * k : 2 * k + 2]) for k in range(2)]
+    strips = first + [job[2:] for job in jobs]
+    needed = list(dict.fromkeys(tile for tile, _ in strips))
+    w_copies = [
+        pltpu.make_async_copy(w.at[tile], tiles.at[k], w_arrived.at[k]) for k, tile in enumerate(needed)
+    ]
+    px_copies = [
+        pltpu.make_async_copy(px.at[tile, :, side, :], pixels.at[k], px_arrived.at[k])
+        for k, (tile, side) in enumerate(strips)
+    ]
+    for copy in px_copies[:2] + w_copies + px_copies[2:]:
+        copy.start()
+    for copy in px_copies[:2] + w_copies[:2]:
+        copy.wait()
+
+    def first_pair(sums):
+        def strips_at(v):
+            weight_a, weight_b = (side_of(tiles, wide, k, k, first[k][1], v) for k in range(2))
+            joint = (weight_a * weight_b).astype(BF16)
+            dense = slice(GROUP * v, GROUP * (v + 1))
+            return [(pixels[k, dense], joint) for k in range(2)]
+
+        strip_products(sums[0], strips_at)
+        for place in range(2):
+            sums_ref[place] = diagonal_sum(pltpu.matmul_pop(sums[0][place]))
+
+    with_sums(first_pair)
+    for k, tile in enumerate(needed):
+        mine = [job for job in jobs if job[2] == tile]
+        if k >= 2:
+            w_copies[k].wait()
+        if mine:
+            wide[k % 2] = tiles[k].astype(F32)
+        for out, n, _, side in mine:
+            out[n, 1] = wide[k % 2, pl.ds(side, CHUNKS, stride=4), :].astype(BF16)
+    for k, (out, n, _, _) in enumerate(jobs):
+        px_copies[2 + k].wait()
+        out[n, 0] = pixels[2 + k].astype(F32).astype(BF16)
+
+
+def packed(px, w):
+    strips = jax.ShapeDtypeStruct((2, 2, CHUNKS, LANES), BF16)
+    tiles = len({t for pair in SENT for t, _ in pair} | {int(INNER[0, 0]), int(INNER[0, 2])})
+    vmem = pl.BlockSpec(memory_space=pltpu.VMEM)
+    return pl.pallas_call(
+        pack_kernel,
+        in_specs=[pl.BlockSpec(memory_space=pl.ANY)] * 2,
+        out_specs=[vmem] * 4,
+        out_shape=[strips] * 3 + [jax.ShapeDtypeStruct((2, 16, 256), F32)],
+        scratch_shapes=[
+            pltpu.VMEM((8, CHUNKS, LANES), I32),
+            pltpu.VMEM((tiles, LINES, LANES), BF16),
+            pltpu.VMEM((2, LINES, LANES), F32),
+            pltpu.SemaphoreType.DMA((8,)),
+            pltpu.SemaphoreType.DMA((tiles,)),
+        ],
+        compiler_params=pltpu.CompilerParams(vmem_limit_bytes=48 << 20),
+        cost_estimate=pl.CostEstimate(flops=1 << 30, bytes_accessed=10 << 20, transcendentals=0),
+    )(px, w)
 
 
 def inner_kernel(table, px, w, out_ref, buffers, tiles, wide, arrived):
@@ -154,7 +177,7 @@
         def finish(pair):
             for place in range(2):
                 rows = slice(16 * pair, 16 * pair + 16)
-                out_ref[place, rows] = diagonal_sum(pltpu.matmul_pop(sums[pair][place]))
+                out_ref[place, rows] = diagonal_sum(pltpu.matmul_pop(sums[pair % 2][place]))
 
         for pair in range(BATCH):
             items = (2 * pair, 2 * pair + 1)
@@ -164,13 +187,14 @@
 
             def strips(v):
                 weight_a, weight_b = (
-                    side_of(tiles, wide, slot, item, entry(table, n, 2 * item + 1), v) for item in items
+                    side_of(tiles.at[slot], wide, item, item % 2, entry(table, n, 2 * item + 1), v)
+                    for item in items
                 )
                 joint = (weight_a * weight_b).astype(BF16)
                 dense = slice(GROUP * v, GROUP * (v + 1))
                 return [(buffers[slot, item, dense], joint) for item in items]
 
-            strip_products(sums[pair], strips)
+            strip_products(sums[pair % 2], strips)
             if pair > 0:
                 finish(pair - 1)
         finish(BATCH - 1)
@@ -179,40 +203,42 @@
 
 
 def inner_sums(px, w):
-    steps = len(INNER) // BATCH
+    count = len(INNER) - 1
+    steps = count // BATCH
     return pl.pallas_call(
-        functools.partial(inner_kernel, INNER.reshape(steps, 4 * BATCH)),
+        functools.partial(inner_kernel, INNER[1:].reshape(steps, 4 * BATCH)),
         grid=(steps,),
         in_specs=[pl.BlockSpec(memory_space=pl.ANY)] * 2,
         out_specs=pl.BlockSpec((2, BATCH * 16, 256), lambda n: (0, n, 0)),
         scratch_shapes=[
             pltpu.VMEM((2, 2 * BATCH, CHUNKS, LANES), I32),
             pltpu.VMEM((2, 2 * BATCH, LINES, LANES), BF16),
-            pltpu.VMEM((2 * BATCH, LINES, LANES), F32),
+            pltpu.VMEM((2, LINES, LANES), F32),
             pltpu.SemaphoreType.DMA((2, 2 * BATCH, 2)),
         ],
-        out_shape=jax.ShapeDtypeStruct((2, len(INNER) * 16, 256), F32),
-        compiler_params=pltpu.CompilerParams(vmem_limit_bytes=VMEM_BYTES),
+        out_shape=jax.ShapeDtypeStruct((2, count * 16, 256), F32),
+        compiler_params=pltpu.CompilerParams(vmem_limit_bytes=48 << 20),
         cost_estimate=pl.CostEstimate(
-            flops=len(INNER) * 4 * 256 * 256 * 8192, bytes_accessed=30 << 20, transcendentals=0
+            flops=count * 4 * 256 * 256 * 8192, bytes_accessed=30 << 20, transcendentals=0
         ),
     )(px, w)
 
 
 def outer_kernel(
-    table, px, w, below, above, left, out_ref, buffers, tiles, wide, arrived
+    table, px, w, below, above, left, start, inner, out_ref, buffers, tiles, wide, arrived
 ):
     n = pl.program_id(0)
-    slot = start_next(BATCH, px, w, table, buffers, tiles, arrived)
+    slot = start_next(OUTER_BATCH, px, w, table, buffers, tiles, arrived)
 
     def steps(sums):
         def finish(pair):
-            own, other = (diagonal_sum(pltpu.matmul_pop(sums[pair][place])) for place in range(2))
-            rows = slice(16 * pair, 16 * pair + 16)
+            own, other = (diagonal_sum(pltpu.matmul_pop(sums[pair % 2][place])) for place in range(2))
+            at = len(INNER) + OUTER_BATCH * n + pair
+            rows = pl.ds(pl.multiple_of(at * 16, 16), 16)
             out_ref[0, rows] = jnp.where(n == 0, own, other)
             out_ref[1, rows] = jnp.where(n == 0, other, own)
 
-        for pair in range(BATCH):
+        for pair in range(OUTER_BATCH):
             for copy in fetch(px, w, table, n, buffers, tiles, arrived, slot, pair):
                 copy.wait()
 
@@ -225,38 +251,43 @@
                         jnp.where(n == 1, above[pair, k, dense], left[pair, k, dense]),
                     ).astype(F32)
 
-                own = side_of(tiles, wide, slot, pair, entry(table, n, 2 * pair + 1), v)
+                own = side_of(tiles.at[slot], wide, pair, pair, entry(table, n, 2 * pair + 1), v)
                 joint = (own * far(1)).astype(BF16)
                 return (buffers[slot, pair, dense], joint), (far(0).astype(I32), joint)
 
-            strip_products(sums[pair], strips)
+            strip_products(sums[pair % 2], strips)
             if pair > 0:
                 finish(pair - 1)
-        finish(BATCH - 1)
+        finish(OUTER_BATCH - 1)
 
     with_sums(steps)
 
-
-def outer_sums(px, w, below, above, left):
+    @pl.when(n == 0)
+    def _():
+        out_ref[:, :16] = start[...]
+        out_ref[:, 16 : len(INNER) * 16] = inner[...]
+
+
+def all_sums(px, w, below, above, left, start, inner):
     count = len(OUTER)
     vmem = pl.BlockSpec(memory_space=pltpu.VMEM)
     return pl.pallas_call(
-        functools.partial(outer_kernel, OUTER.reshape(count // BATCH, 2 * BATCH)),
-        grid=(count // BATCH,),
-        in_specs=[pl.BlockSpec(memory_space=pl.ANY)] * 2 + [vmem] * 3,
-        out_specs=pl.BlockSpec((2, BATCH * 16, 256), lambda n: (0, n, 0)),
+        functools.partial(outer_kernel, OUTER.reshape(count // OUTER_BATCH, 2 * OUTER_BATCH)),
+        grid=(count // OUTER_BATCH,),
+        in_specs=[pl.BlockSpec(memory_space=pl.ANY)] * 2 + [vmem] * 5,
+        out_specs=vmem,
         scratch_shapes=[
-            pltpu.VMEM((2, BATCH, CHUNKS, LANES), I32),
-            pltpu.VMEM((2, BATCH, LINES, LANES), BF16),
-            pltpu.VMEM((BATCH, LINES, LANES), F32),
-            pltpu.SemaphoreType.DMA((2, BATCH, 2)),
+            pltpu.VMEM((2, OUTER_BATCH, CHUNKS, LANES), I32),
+            pltpu.VMEM((2, OUTER_BATCH, LINES, LANES), BF16),
+            pltpu.VMEM((OUTER_BATCH, LINES, LANES), F32),
+            pltpu.SemaphoreType.DMA((2, OUTER_BATCH, 2)),
         ],
-        out_shape=jax.ShapeDtypeStruct((2, count * 16, 256), F32),
-        compiler_params=pltpu.CompilerParams(vmem_limit_bytes=VMEM_BYTES),
+        out_shape=jax.ShapeDtypeStruct((2, (len(INNER) + count) * 16, 256), F32),
+        compiler_params=pltpu.CompilerParams(vmem_limit_bytes=48 << 20),
         cost_estimate=pl.CostEstimate(
             flops=count * 4 * 256 * 256 * 8192, bytes_accessed=9 << 20, transcendentals=0
         ),
-    )(px, w, below, above, left)
+    )(px, w, below, above, left, start, inner)
 
 
 def pieces(x):
@@ -307,18 +338,17 @@
     return jnp.sum(jnp.where(total > 0, spread, 0.0), axis=0, keepdims=True)
 
 
-def results_kernel(inner, outer, out_ref):
-    first, second = (jnp.concatenate([inner[k], outer[k]], 0) for k in range(2))
-    out_ref[...] = jnp.broadcast_to(pair_results(first, second), out_ref.shape)
-
-
-def results(inner, outer, devices):
+def results_kernel(sums, out_ref):
+    out_ref[...] = jnp.broadcast_to(pair_results(sums[0], sums[1]), out_ref.shape)
+
+
+def results(sums, devices):
     return pl.pallas_call(
         results_kernel,
-        in_specs=[pl.BlockSpec(memory_space=pltpu.VMEM)] * 2,
+        in_specs=[pl.BlockSpec(memory_space=pltpu.VMEM)],
         out_specs=pl.BlockSpec(memory_space=pltpu.VMEM),
         out_shape=jax.ShapeDtypeStruct((devices, LANES), F32),
-    )(inner, outer)
+    )(sums)
 
 
 def on_grid(gathered, height, count_y):
@@ -346,10 +376,13 @@
     return apply(place, jnp.concatenate(parts, 0))
 
 
-def sweep_kernel(height, width, count_y, where_ref, gathered, adjacency, out_ref, links, gain_ref):
+def sweep_kernel(height, width, count_y, where_ref, gathered, adjacency, out_ref, held, links, gain_ref, arrived):
+    copy = pltpu.make_async_copy(adjacency, held, arrived)
+    copy.start()
     grid = on_grid(gathered[...], height, count_y)
     links[...] = jnp.zeros_like(links)
-    links[:, :, :width] = adjacency[...]
+    copy.wait()
+    links[:, :, :width] = held[...]
     row = lax.broadcasted_iota(I32, (height, LANES), 0)
     column = lax.broadcasted_iota(I32, (height, LANES), 1)
     below = (links[1] > 0) & (row < height - 1) & (column < width)
@@ -374,21 +407,26 @@
     a_up, a_down, a_left, a_right = (scale * a for a in (conf_up, conf_down, conf_left, conf_right))
 
     ones = a_up + a_down + a_left + a_right
+    columns = down(a_up) + up(a_down) + rights(a_left) + lefts(a_right)
 
     def mean(a):
-        columns = jnp.sum(a, axis=0, keepdims=True)
-        return jnp.sum(columns, axis=1, keepdims=True) * (1.0 / (height * width))
-
-    def sweep(_, fresh):
+        by_column = jnp.sum(a, axis=0, keepdims=True)
+        return jnp.sum(by_column, axis=1, keepdims=True) * (1.0 / (height * width))
+
+    mean_constant, mean_ones = mean(constant), mean(ones)
+
+    def sweep(_, state):
+        fresh, average = state
         spread = (
             (a_up * up(fresh) + a_down * down(fresh))
             + (a_left * lefts(fresh) + a_right * rights(fresh))
             + constant
         )
-        return spread - mean(fresh) * ones
-
-    fresh = lax.fori_loop(0, ITERS - 1, sweep, constant, unroll=True)
-    gain = fresh - mean(fresh)
+        later = mean(columns * fresh) + (mean_constant - average * mean_ones)
+        return spread - average * ones, later
+
+    fresh, average = lax.fori_loop(0, ITERS - 1, sweep, (constant, mean_constant), unroll=True)
+    gain = fresh - average
     gain_ref[...] = pltpu.roll(gain, LANES - where_ref[1] * COLS, 1)
     out_ref[...] = gain_ref[pl.ds(where_ref[0] * ROWS, ROWS), :COLS]
 
@@ -400,11 +438,17 @@
         in_specs=[
             pl.BlockSpec(memory_space=pltpu.SMEM),
             pl.BlockSpec(memory_space=pltpu.VMEM),
-            pl.BlockSpec(memory_space=pltpu.VMEM),
+            pl.BlockSpec(memory_space=pl.ANY),
         ],
         out_specs=pl.BlockSpec(memory_space=pltpu.VMEM),
         out_shape=jax.ShapeDtypeStruct((ROWS, COLS), F32),
-        scratch_shapes=[pltpu.VMEM((2, height, LANES), I32), pltpu.VMEM((height, LANES), F32)],
+        scratch_shapes=[
+            pltpu.VMEM(adjacency.shape, I32),
+            pltpu.VMEM((2, height, LANES), I32),
+            pltpu.VMEM((height, LANES), F32),
+            pltpu.SemaphoreType.DMA,
+        ],
+        compiler_params=pltpu.CompilerParams(vmem_limit_bytes=56 << 20),
     )(where, gathered, adjacency)
 
 
@@ -415,13 +459,13 @@
     count_x, count_y = lax.axis_size("gx"), lax.axis_size("gy")
     ahead = lambda n: [(i, i + 1) for i in range(n - 1)]
     back = lambda n: [(i + 1, i) for i in range(n - 1)]
-    below, above, left = packed(px, w)
+    below, above, left, start = packed(px, w)
     below = lax.ppermute(below, "gy", back(count_y))
     above = lax.ppermute(above, "gy", ahead(count_y))
     left = lax.ppermute(left, "gx", ahead(count_x))
     inner = inner_sums(px, w)
-    outer = outer_sums(px, w, below, above, left)
-    gathered = lax.all_to_all(results(inner, outer, count_x * count_y), ALL, 0, 0, tiled=True)
+    sums = all_sums(px, w, below, above, left, start, inner)
+    gathered = lax.all_to_all(results(sums, count_x * count_y), ALL, 0, 0, tiled=True)
     where = jnp.stack([lax.axis_index("gy"), lax.axis_index("gx")]).astype(I32)
     return sweeps(gathered, adjacency, where)
 

time: 88.3 us -> 87.8 us (level)
    pallas_call x2, Pallas kernels: 43 us -> 40.5 us  [the longest x1 23.4 us: inner_sums(): pl.pallas_call(functools.partial(inner_kernel, INNER[1:].reshape(steps, 4...]
    pallas_call x1, Pallas kernels: 5.04 us -> 7.14 us  [packed(): pl.pallas_call(pack_kernel, in_specs=[pl.BlockSpec(memory_space=pl.ANY)]...]
    unnamed x6 -> x4, local copies, waits for them, and re-layouts: 2.01 us -> 1.4 us
  transfers between devices with their start and end apart: 4 -> 4, of which waited for: 1 -> 1; matrix products, arithmetic and copies ran while one was open for 1% -> 1% of each run, Pallas kernels for 29% -> 27%
where the time goes in v2:
time: 87.8 us; the launch traced here: 87.5 us
  Pallas kernels  53.9 us (61%)
  starting transfers between devices  22.1 us (25%)
  waiting for transfers between devices  9.12 us (10%)
  local copies, waits for them, and re-layouts  1.4 us (2%)
    pallas_call x1, Pallas kernels, inner_sums(): pl.pallas_call(functools.partial(inner_kernel, INNER[1:].reshape(steps, 4...  23.4 us
    pallas_call x1, Pallas kernels, all_sums(): pl.pallas_call(functools.partial(outer_kernel, OUTER.reshape(count // OUT...  17.1 us
    all_to_all x1, starting transfers between devices, body(): lax.all_to_all(results(sums, count_x * count_y), ALL, 0, 0, tiled=True)  11.4 us
    all_to_all x1, waiting for transfers between devices, body(): lax.all_to_all(results(sums, count_x * count_y), ALL, 0, 0, tiled=True)  9.11 us
    pallas_call x1, Pallas kernels, packed(): pl.pallas_call(pack_kernel, in_specs=[pl.BlockSpec(memory_space=pl.ANY)]...  7.14 us
    ppermute x1, starting transfers between devices, body(): left = lax.ppermute(left, 'gx', ahead(count_x))  4.75 us
    ppermute x1, starting transfers between devices, body(): above = lax.ppermute(above, 'gy', ahead(count_y))  4.64 us
    pallas_call x1, Pallas kernels, sweeps(): pl.pallas_call(functools.partial(sweep_kernel, height, width, height // R...  3.91 us
  transfers between devices with their start and end apart: 4, of which 1 were waited for; matrix products, arithmetic and copies ran while one was open for 1% of the time, Pallas kernels for 27%

profile of v2, /device:TPU:1, one launch (start us, length us, event | category | flops | bytes accessed | tf_op | source)
XLA Modules:
  0.0 87.5 jit_solution(5409238771439608319)
XLA Ops:
  0.0 7.1 %shard_map.37 = (bf16[2,2,1024,128]{3,2,1,0:T(8,128)(2,1)}, bf16[2,2,1024,128]{3,2,1,0:T(8,128)(2,1)}, bf16[2,2,1024,128]{3,2,1,0:T(8,128)(2,1)S(1)}, f32[2,16,256]{2,1,0:T(8,128)S(1)}) custom-call(s32[8,1024,4,128]{3,2,1,0:T(4,128)} %bitcast.14, bf16[8,4096,128]{2,1,0:T(8,128)(2,1)} %bitcast.17), custom_call_target="tpu_custom_call" | custom-call | flops 1073741824 | bytes 10485760 | tf_op jit(solution)/shard_map/pallas_call | solution.py:155
  7.2 1.3 %collective-permute-start = (bf16[2,2,1024,128]{3,2,1,0:T(8,128)(2,1)}, bf16[2,2,1024,128]{3,2,1,0:T(8,128)(2,1)S(1)}, u32[]{:S(2)}, u32[]{:S(2)}) collective-permute-start(bf16[2,2,1024,128]{3,2,1,0:T(8,128)(2,1)} %get-tuple-element.9), channel_id=1, source_target_pairs={{1,0},{2,1},{3,2},{4,3},{5,4},{6,5},{7,6},{8,7},{9,8},{10,9},{11,1... | collective-permute-start | bytes 3145736 | tf_op jit(solution)/shard_map/ppermute | solution.py:463
  8.5 4.6 %collective-permute-start.1 = (bf16[2,2,1024,128]{3,2,1,0:T(8,128)(2,1)}, bf16[2,2,1024,128]{3,2,1,0:T(8,128)(2,1)S(1)}, u32[]{:S(2)}, u32[]{:S(2)}) collective-permute-start(bf16[2,2,1024,128]{3,2,1,0:T(8,128)(2,1)} %get-tuple-element.10), channel_id=1, source_target_pairs={{0,1},{1,2},{2,3},{3,4},{4,5},{5,6},{6,7},{7,8},{8,9},{9,10},{10,1... | collective-permute-start | bytes 3145736 | tf_op jit(solution)/shard_map/ppermute | solution.py:464
  13.1 4.8 %collective-permute-start.2 = (bf16[2,2,1024,128]{3,2,1,0:T(8,128)(2,1)S(1)}, bf16[2,2,1024,128]{3,2,1,0:T(8,128)(2,1)}, u32[]{:S(2)}, u32[]{:S(2)}) collective-permute-start(bf16[2,2,1024,128]{3,2,1,0:T(8,128)(2,1)S(1)} %get-tuple-element.11), channel_id=1, source_target_pairs={{0,16},{16,32},{32,48},{48,64},{64,80},{80,96},{96,112},{1,17},{17... | collective-permute-start | bytes 3145736 | tf_op jit(solution)/shard_map/ppermute | solution.py:465
  17.9 23.4 %shard_map.38.inner = f32[2,144,256]{2,1,0:T(8,128)S(1)} custom-call(s32[8,1024,4,128]{3,2,1,0:T(4,128)} %bitcast.15, bf16[8,4096,128]{2,1,0:T(8,128)(2,1)} %bitcast.18), custom_call_target="tpu_custom_call" | custom-call | flops 19327352832 | bytes 31457280 | tf_op jit(solution)/shard_map/pallas_call | solution.py:208
  41.3 0.0 collective-permute-done.below
  41.3 0.0 collective-permute-done.1.above
  41.3 0.0 collective-permute-done.2.left
  41.3 17.1 %shard_map.39.sums = f32[2,256,256]{2,1,0:T(8,128)S(1)} custom-call(s32[8,1024,4,128]{3,2,1,0:T(4,128)} %bitcast.16, bf16[8,4096,128]{2,1,0:T(8,128)(2,1)} %bitcast.19, bf16[2,2,1024,128]{3,2,1,0:T(8,128)(2,1)S(1)} %collective-permute-done.below, bf16[2,2,1024,128]{3,2,1,0:T(8,128)(2,1)S(1)} %collective-permute-done.1.above, ...), custom_call_target="tpu_custom_call" | custom-call | flops 12884901888 | bytes 9437184 | tf_op jit(solution)/shard_map/pallas_call | solution.py:274
  58.4 0.0 copy-start
  58.4 0.8 copy-done
  59.2 2.4 %shard_map.40 = f32[128,128]{1,0:T(8,128)} custom-call(f32[2,256,256]{2,1,0:T(8,128)} %copy-done), custom_call_target="tpu_custom_call" | custom-call | tf_op jit(solution)/shard_map/pallas_call | solution.py:346
  61.6 11.4 %all-to-all-start = ((f32[128,1,128]{2,1,0:T(1,128)}), f32[128,1,128]{2,1,0:T(1,128)S(1)}, u32[]{:S(2)}, u32[]{:S(2)}) async-start(f32[128,1,128]{2,1,0:T(1,128)} %bitcast.20), calls=%async_computation | async-start | bytes 131072 | tf_op jit(solution)/shard_map/all_to_all | solution.py:468
  73.0 0.7 pad_add_fusion.where_ref
  73.7 9.1 %all-to-all-done = f32[128,1,128]{2,1,0:T(1,128)S(1)} async-done(((f32[128,1,128]{2,1,0:T(1,128)}), f32[128,1,128]{2,1,0:T(1,128)S(1)}, u32[]{:S(2)}, u32[]{:S(2)}) %all-to-all-start) | async-done | bytes 65568 | tf_op jit(solution)/shard_map/all_to_all | solution.py:468
  82.8 0.0 copy-start.1
  82.8 0.6 copy-done.1
  83.4 3.9 %shard_map.41 = f32[2,4]{1,0:T(2,128)} custom-call(s32[2]{0:T(128)} %pad_add_fusion.where_ref, f32[128,128]{1,0:T(8,128)} %bitcast.21, s32[2,32,32]{2,1,0:T(8,128)} %adjacency.1), custom_call_target="tpu_custom_call" | custom-call | tf_op jit(solution)/shard_map/pallas_call | solution.py:436
Async XLA Ops:
  7.2 34.2 %collective-permute-start = (bf16[2,2,1024,128]{3,2,1,0:T(8,128)(2,1)}, bf16[2,2,1024,128]{3,2,1,0:T(8,128)(2,1)S(1)}, u32[]{:S(2)}, u32[]{:S(2)}) collective-permute-start(bf16[2,2,1024,128]{3,2,1,0:T(8,128)(2,1)} %get-tuple-element.9), channel_id=1, source_target_pairs={{1,0},{2,1},{3,2},{4,3},{5,4},{6,5},{7,6},{8,7},{9,8},{10,9},{11,1... | collective-permute-start | bytes 3145736 | tf_op jit(solution)/shard_map/ppermute | solution.py:463
  8.5 32.9 %collective-permute-start.1 = (bf16[2,2,1024,128]{3,2,1,0:T(8,128)(2,1)}, bf16[2,2,1024,128]{3,2,1,0:T(8,128)(2,1)S(1)}, u32[]{:S(2)}, u32[]{:S(2)}) collective-permute-start(bf16[2,2,1024,128]{3,2,1,0:T(8,128)(2,1)} %get-tuple-element.10), channel_id=1, source_target_pairs={{0,1},{1,2},{2,3},{3,4},{4,5},{5,6},{6,7},{7,8},{8,9},{9,10},{10,1... | collective-permute-start | bytes 3145736 | tf_op jit(solution)/shard_map/ppermute | solution.py:464
  13.1 28.2 %collective-permute-start.2 = (bf16[2,2,1024,128]{3,2,1,0:T(8,128)(2,1)S(1)}, bf16[2,2,1024,128]{3,2,1,0:T(8,128)(2,1)}, u32[]{:S(2)}, u32[]{:S(2)}) collective-permute-start(bf16[2,2,1024,128]{3,2,1,0:T(8,128)(2,1)S(1)} %get-tuple-element.11), channel_id=1, source_target_pairs={{0,16},{16,32},{32,48},{48,64},{64,80},{80,96},{96,112},{1,17},{17... | collective-permute-start | bytes 3145736 | tf_op jit(solution)/shard_map/ppermute | solution.py:465
  58.4 0.8 copy-start
  61.6 21.2 %all-to-all-start = ((f32[128,1,128]{2,1,0:T(1,128)}), f32[128,1,128]{2,1,0:T(1,128)S(1)}, u32[]{:S(2)}, u32[]{:S(2)}) async-start(f32[128,1,128]{2,1,0:T(1,128)} %bitcast.20), calls=%async_computation | async-start | bytes 131072 | tf_op jit(solution)/shard_map/all_to_all | solution.py:468
  82.8 0.6 copy-start.1

commit v3 on v2

--- a/solution.py
+++ b/solution.py
@@ -12,7 +12,7 @@
 ROWS, COLS = 2, 4
 CHUNKS, LANES = 1024, 128
 LINES = 4 * CHUNKS
-BATCH = 3
+BATCH = 2
 OUTER_BATCH = 2
 GROUP = 16
 ALL = ("gx", "gy")
@@ -104,68 +104,45 @@
     return wide[room, pl.ds(o + side, GROUP, stride=4), :]
 
 
-def pack_kernel(
-    px, w, below_ref, above_ref, left_ref, sums_ref, pixels, tiles, wide, px_arrived, w_arrived
-):
+def pack_kernel(px, w, below_ref, above_ref, left_ref, pixels, tiles, wide, px_arrived, w_arrived):
     jobs = [(out, n) + SENT[k][n] for k, out in enumerate((below_ref, above_ref, left_ref)) for n in range(2)]
-    first = [tuple(int(v) for v in INNER[0, 2 * k : 2 * k + 2]) for k in range(2)]
-    strips = first + [job[2:] for job in jobs]
-    needed = list(dict.fromkeys(tile for tile, _ in strips))
+    needed = sorted({job[2] for job in jobs}, key=[job[2] for job in jobs].index)
     w_copies = [
         pltpu.make_async_copy(w.at[tile], tiles.at[k], w_arrived.at[k]) for k, tile in enumerate(needed)
     ]
     px_copies = [
-        pltpu.make_async_copy(px.at[tile, :, side, :], pixels.at[k], px_arrived.at[k])
-        for k, (tile, side) in enumerate(strips)
+        pltpu.make_async_copy(px.at[job[2], :, job[3], :], pixels.at[k], px_arrived.at[k])
+        for k, job in enumerate(jobs)
     ]
-    for copy in px_copies[:2] + w_copies + px_copies[2:]:
+    for copy in w_copies + px_copies:
         copy.start()
-    for copy in px_copies[:2] + w_copies[:2]:
-        copy.wait()
-
-    def first_pair(sums):
-        def strips_at(v):
-            weight_a, weight_b = (side_of(tiles, wide, k, k, first[k][1], v) for k in range(2))
-            joint = (weight_a * weight_b).astype(BF16)
-            dense = slice(GROUP * v, GROUP * (v + 1))
-            return [(pixels[k, dense], joint) for k in range(2)]
-
-        strip_products(sums[0], strips_at)
-        for place in range(2):
-            sums_ref[place] = diagonal_sum(pltpu.matmul_pop(sums[0][place]))
-
-    with_sums(first_pair)
     for k, tile in enumerate(needed):
-        mine = [job for job in jobs if job[2] == tile]
-        if k >= 2:
-            w_copies[k].wait()
-        if mine:
-            wide[k % 2] = tiles[k].astype(F32)
-        for out, n, _, side in mine:
+        w_copies[k].wait()
+        wide[k % 2] = tiles[k].astype(F32)
+        for out, n, _, side in (job for job in jobs if job[2] == tile):
             out[n, 1] = wide[k % 2, pl.ds(side, CHUNKS, stride=4), :].astype(BF16)
     for k, (out, n, _, _) in enumerate(jobs):
-        px_copies[2 + k].wait()
-        out[n, 0] = pixels[2 + k].astype(F32).astype(BF16)
+        px_copies[k].wait()
+        out[n, 0] = pixels[k].astype(F32).astype(BF16)
 
 
 def packed(px, w):
     strips = jax.ShapeDtypeStruct((2, 2, CHUNKS, LANES), BF16)
-    tiles = len({t for pair in SENT for t, _ in pair} | {int(INNER[0, 0]), int(INNER[0, 2])})
     vmem = pl.BlockSpec(memory_space=pltpu.VMEM)
     return pl.pallas_call(
         pack_kernel,
         in_specs=[pl.BlockSpec(memory_space=pl.ANY)] * 2,
-        out_specs=[vmem] * 4,
-        out_shape=[strips] * 3 + [jax.ShapeDtypeStruct((2, 16, 256), F32)],
+        out_specs=[vmem] * 3,
+        out_shape=[strips] * 3,
         scratch_shapes=[
-            pltpu.VMEM((8, CHUNKS, LANES), I32),
-            pltpu.VMEM((tiles, LINES, LANES), BF16),
+            pltpu.VMEM((6, CHUNKS, LANES), I32),
+            pltpu.VMEM((5, LINES, LANES), BF16),
             pltpu.VMEM((2, LINES, LANES), F32),
-            pltpu.SemaphoreType.DMA((8,)),
-            pltpu.SemaphoreType.DMA((tiles,)),
+            pltpu.SemaphoreType.DMA((6,)),
+            pltpu.SemaphoreType.DMA((5,)),
         ],
         compiler_params=pltpu.CompilerParams(vmem_limit_bytes=48 << 20),
-        cost_estimate=pl.CostEstimate(flops=1 << 30, bytes_accessed=10 << 20, transcendentals=0),
+        cost_estimate=pl.CostEstimate(flops=1 << 20, bytes_accessed=8 << 20, transcendentals=0),
     )(px, w)
 
 
@@ -203,10 +180,10 @@
 
 
 def inner_sums(px, w):
-    count = len(INNER) - 1
+    count = len(INNER)
     steps = count // BATCH
     return pl.pallas_call(
-        functools.partial(inner_kernel, INNER[1:].reshape(steps, 4 * BATCH)),
+        functools.partial(inner_kernel, INNER.reshape(steps, 4 * BATCH)),
         grid=(steps,),
         in_specs=[pl.BlockSpec(memory_space=pl.ANY)] * 2,
         out_specs=pl.BlockSpec((2, BATCH * 16, 256), lambda n: (0, n, 0)),
@@ -225,10 +202,17 @@
 
 
 def outer_kernel(
-    table, px, w, below, above, left, start, inner, out_ref, buffers, tiles, wide, arrived
+    table, px, w, below, above, left, inner, out_ref, buffers, tiles, wide, arrived, received, staged
 ):
     n = pl.program_id(0)
+    for step, source in enumerate((below, above, left)):
+
+        @pl.when(n == step)
+        def _(source=source):
+            pltpu.make_async_copy(source, received, staged).start()
+
     slot = start_next(OUTER_BATCH, px, w, table, buffers, tiles, arrived)
+    pltpu.make_async_copy(below, received, staged).wait()
 
     def steps(sums):
         def finish(pair):
@@ -245,15 +229,10 @@
             def strips(v):
                 dense = slice(GROUP * v, GROUP * (v + 1))
 
-                def far(k):
-                    return jnp.where(
-                        n == 0, below[pair, k, dense],
-                        jnp.where(n == 1, above[pair, k, dense], left[pair, k, dense]),
-                    ).astype(F32)
-
                 own = side_of(tiles.at[slot], wide, pair, pair, entry(table, n, 2 * pair + 1), v)
-                joint = (own * far(1)).astype(BF16)
-                return (buffers[slot, pair, dense], joint), (far(0).astype(I32), joint)
+                joint = (own * received[pair, 1, dense].astype(F32)).astype(BF16)
+                far = received[pair, 0, dense].astype(F32).astype(I32)
+                return (buffers[slot, pair, dense], joint), (far, joint)
 
             strip_products(sums[pair % 2], strips)
             if pair > 0:
@@ -264,30 +243,31 @@
 
     @pl.when(n == 0)
     def _():
-        out_ref[:, :16] = start[...]
-        out_ref[:, 16 : len(INNER) * 16] = inner[...]
-
-
-def all_sums(px, w, below, above, left, start, inner):
+        out_ref[:, : len(INNER) * 16] = inner[...]
+
+
+def all_sums(px, w, below, above, left, inner):
     count = len(OUTER)
     vmem = pl.BlockSpec(memory_space=pltpu.VMEM)
     return pl.pallas_call(
         functools.partial(outer_kernel, OUTER.reshape(count // OUTER_BATCH, 2 * OUTER_BATCH)),
         grid=(count // OUTER_BATCH,),
-        in_specs=[pl.BlockSpec(memory_space=pl.ANY)] * 2 + [vmem] * 5,
+        in_specs=[pl.BlockSpec(memory_space=pl.ANY)] * 2 + [vmem] * 4,
         out_specs=vmem,
         scratch_shapes=[
             pltpu.VMEM((2, OUTER_BATCH, CHUNKS, LANES), I32),
             pltpu.VMEM((2, OUTER_BATCH, LINES, LANES), BF16),
             pltpu.VMEM((OUTER_BATCH, LINES, LANES), F32),
             pltpu.SemaphoreType.DMA((2, OUTER_BATCH, 2)),
+            pltpu.VMEM(below.shape, BF16),
+            pltpu.SemaphoreType.DMA,
         ],
         out_shape=jax.ShapeDtypeStruct((2, (len(INNER) + count) * 16, 256), F32),
         compiler_params=pltpu.CompilerParams(vmem_limit_bytes=48 << 20),
         cost_estimate=pl.CostEstimate(
             flops=count * 4 * 256 * 256 * 8192, bytes_accessed=9 << 20, transcendentals=0
         ),
-    )(px, w, below, above, left, start, inner)
+    )(px, w, below, above, left, inner)
 
 
 def pieces(x):
@@ -348,6 +328,7 @@
         in_specs=[pl.BlockSpec(memory_space=pltpu.VMEM)],
         out_specs=pl.BlockSpec(memory_space=pltpu.VMEM),
         out_shape=jax.ShapeDtypeStruct((devices, LANES), F32),
+        compiler_params=pltpu.CompilerParams(vmem_limit_bytes=16 << 20),
     )(sums)
 
 
@@ -448,7 +429,7 @@
             pltpu.VMEM((height, LANES), F32),
             pltpu.SemaphoreType.DMA,
         ],
-        compiler_params=pltpu.CompilerParams(vmem_limit_bytes=56 << 20),
+        compiler_params=pltpu.CompilerParams(vmem_limit_bytes=8 << 20),
     )(where, gathered, adjacency)
 
 
@@ -459,12 +440,12 @@
     count_x, count_y = lax.axis_size("gx"), lax.axis_size("gy")
     ahead = lambda n: [(i, i + 1) for i in range(n - 1)]
     back = lambda n: [(i + 1, i) for i in range(n - 1)]
-    below, above, left, start = packed(px, w)
+    below, above, left = packed(px, w)
     below = lax.ppermute(below, "gy", back(count_y))
     above = lax.ppermute(above, "gy", ahead(count_y))
     left = lax.ppermute(left, "gx", ahead(count_x))
     inner = inner_sums(px, w)
-    sums = all_sums(px, w, below, above, left, start, inner)
+    sums = all_sums(px, w, below, above, left, inner)
     gathered = lax.all_to_all(results(sums, count_x * count_y), ALL, 0, 0, tiled=True)
     where = jnp.stack([lax.axis_index("gy"), lax.axis_index("gx")]).astype(I32)
     return sweeps(gathered, adjacency, where)

time: 87.8 us -> 84.9 us (0.967)
  local copies, waits for them, and re-layouts: 1.4 us -> 0.01 us
  Pallas kernels: 53.9 us -> 52.9 us
    pallas_call x1, Pallas kernels: 23.4 us -> 25.9 us  [inner_sums(): pl.pallas_call(functools.partial(inner_kernel, INNER.reshape(steps, 4 * B...]
    pallas_call x1, Pallas kernels: 7.14 us -> 5.05 us  [packed(): pl.pallas_call(pack_kernel, in_specs=[pl.BlockSpec(memory_space=pl.ANY)]...]
    unnamed x4 -> x2, local copies, waits for them, and re-layouts: 1.4 us -> 0.01 us
    pallas_call x1, Pallas kernels: 2.36 us -> 1.34 us  [results(): pl.pallas_call(results_kernel, in_specs=[pl.BlockSpec(memory_space=pltpu....]
  transfers between devices with their start and end apart: 4 -> 4, of which waited for: 1 -> 1; matrix products, arithmetic and copies ran while one was open for 1% -> 0% of each run, Pallas kernels for 27% -> 31%
where the time goes in v3:
time: 84.9 us; the launch traced here: 84.7 us
  Pallas kernels  52.9 us (62%)
  starting transfers between devices  21.9 us (26%)
  waiting for transfers between devices  9.71 us (11%)
    pallas_call x1, Pallas kernels, inner_sums(): pl.pallas_call(functools.partial(inner_kernel, INNER.reshape(steps, 4 * B...  25.9 us
    pallas_call x1, Pallas kernels, all_sums(): pl.pallas_call(functools.partial(outer_kernel, OUTER.reshape(count // OUT...  17.3 us
    all_to_all x1, starting transfers between devices, body(): lax.all_to_all(results(sums, count_x * count_y), ALL, 0, 0, tiled=True)  11.4 us
    all_to_all x1, waiting for transfers between devices, body(): lax.all_to_all(results(sums, count_x * count_y), ALL, 0, 0, tiled=True)  9.7 us
    pallas_call x1, Pallas kernels, packed(): pl.pallas_call(pack_kernel, in_specs=[pl.BlockSpec(memory_space=pl.ANY)]...  5.05 us
    ppermute x1, starting transfers between devices, body(): above = lax.ppermute(above, 'gy', ahead(count_y))  4.64 us
    ppermute x1, starting transfers between devices, body(): left = lax.ppermute(left, 'gx', ahead(count_x))  4.57 us
    pallas_call x1, Pallas kernels, sweeps(): pl.pallas_call(functools.partial(sweep_kernel, height, width, height // R...  3.29 us
  transfers between devices with their start and end apart: 4, of which 1 were waited for; matrix products, arithmetic and copies ran while one was open for 0% of the time, Pallas kernels for 31%

profile of v3, /device:TPU:1, one launch (start us, length us, event | category | flops | bytes accessed | tf_op | source)
XLA Modules:
  0.0 84.7 jit_solution(18051602327139081263)
XLA Ops:
  0.0 5.0 %shard_map.37 = (bf16[2,2,1024,128]{3,2,1,0:T(8,128)(2,1)}, bf16[2,2,1024,128]{3,2,1,0:T(8,128)(2,1)}, bf16[2,2,1024,128]{3,2,1,0:T(8,128)(2,1)S(1)}) custom-call(s32[8,1024,4,128]{3,2,1,0:T(4,128)} %bitcast.15, bf16[8,4096,128]{2,1,0:T(8,128)(2,1)} %bitcast.18), custom_call_target="tpu_custom_call" | custom-call | flops 1048576 | bytes 8388608 | tf_op jit(solution)/shard_map/pallas_call | solution.py:132
  5.1 1.3 %collective-permute-start = (bf16[2,2,1024,128]{3,2,1,0:T(8,128)(2,1)}, bf16[2,2,1024,128]{3,2,1,0:T(8,128)(2,1)S(1)}, u32[]{:S(2)}, u32[]{:S(2)}) collective-permute-start(bf16[2,2,1024,128]{3,2,1,0:T(8,128)(2,1)} %get-tuple-element.8), channel_id=1, source_target_pairs={{1,0},{2,1},{3,2},{4,3},{5,4},{6,5},{7,6},{8,7},{9,8},{10,9},{11,1... | collective-permute-start | bytes 3145736 | tf_op jit(solution)/shard_map/ppermute | solution.py:444
  6.4 4.6 %collective-permute-start.1 = (bf16[2,2,1024,128]{3,2,1,0:T(8,128)(2,1)}, bf16[2,2,1024,128]{3,2,1,0:T(8,128)(2,1)S(1)}, u32[]{:S(2)}, u32[]{:S(2)}) collective-permute-start(bf16[2,2,1024,128]{3,2,1,0:T(8,128)(2,1)} %get-tuple-element.9), channel_id=1, source_target_pairs={{0,1},{1,2},{2,3},{3,4},{4,5},{5,6},{6,7},{7,8},{8,9},{9,10},{10,1... | collective-permute-start | bytes 3145736 | tf_op jit(solution)/shard_map/ppermute | solution.py:445
  11.0 4.6 %collective-permute-start.2 = (bf16[2,2,1024,128]{3,2,1,0:T(8,128)(2,1)S(1)}, bf16[2,2,1024,128]{3,2,1,0:T(8,128)(2,1)}, u32[]{:S(2)}, u32[]{:S(2)}) collective-permute-start(bf16[2,2,1024,128]{3,2,1,0:T(8,128)(2,1)S(1)} %get-tuple-element.10), channel_id=1, source_target_pairs={{0,16},{16,32},{32,48},{48,64},{64,80},{80,96},{96,112},{1,17},{17... | collective-permute-start | bytes 3145736 | tf_op jit(solution)/shard_map/ppermute | solution.py:446
  15.6 25.9 %shard_map.38.inner = f32[2,160,256]{2,1,0:T(8,128)S(1)} custom-call(s32[8,1024,4,128]{3,2,1,0:T(4,128)} %bitcast.16, bf16[8,4096,128]{2,1,0:T(8,128)(2,1)} %bitcast.19), custom_call_target="tpu_custom_call" | custom-call | flops 21474836480 | bytes 31457280 | tf_op jit(solution)/shard_map/pallas_call | solution.py:185
  41.5 0.0 copy-start
  41.5 0.0 collective-permute-done.below
  41.6 0.0 collective-permute-done.1.above
  41.6 0.0 collective-permute-done.2.left
  41.6 17.3 %shard_map.39.sums = f32[2,256,256]{2,1,0:T(8,128)S(1)} custom-call(s32[8,1024,4,128]{3,2,1,0:T(4,128)} %bitcast.17, bf16[8,4096,128]{2,1,0:T(8,128)(2,1)} %bitcast.20, bf16[2,2,1024,128]{3,2,1,0:T(8,128)(2,1)S(1)} %collective-permute-done.below, bf16[2,2,1024,128]{3,2,1,0:T(8,128)(2,1)S(1)} %collective-permute-done.1.above, ...), custom_call_target="tpu_custom_call" | custom-call | flops 12884901888 | bytes 9437184 | tf_op jit(solution)/shard_map/pallas_call | solution.py:252
  58.9 1.3 %shard_map.40 = f32[128,128]{1,0:T(8,128)} custom-call(f32[2,256,256]{2,1,0:T(8,128)S(1)} %shard_map.39.sums), custom_call_target="tpu_custom_call" | custom-call | tf_op jit(solution)/shard_map/pallas_call | solution.py:326
  60.2 11.4 %all-to-all-start = ((f32[128,1,128]{2,1,0:T(1,128)}), f32[128,1,128]{2,1,0:T(1,128)S(1)}, u32[]{:S(2)}, u32[]{:S(2)}) async-start(f32[128,1,128]{2,1,0:T(1,128)} %bitcast.11), calls=%async_computation | async-start | bytes 131072 | tf_op jit(solution)/shard_map/all_to_all | solution.py:449
  71.6 0.1 pad_add_fusion.where_ref
  71.7 9.7 %all-to-all-done = f32[128,1,128]{2,1,0:T(1,128)S(1)} async-done(((f32[128,1,128]{2,1,0:T(1,128)}), f32[128,1,128]{2,1,0:T(1,128)S(1)}, u32[]{:S(2)}, u32[]{:S(2)}) %all-to-all-start) | async-done | bytes 65568 | tf_op jit(solution)/shard_map/all_to_all | solution.py:449
  81.4 0.0 copy-done
  81.4 3.3 %shard_map.41 = f32[2,4]{1,0:T(2,128)} custom-call(s32[2]{0:T(128)S(1)} %pad_add_fusion.where_ref, f32[128,128]{1,0:T(8,128)S(1)} %bitcast.14, s32[2,32,32]{2,1,0:T(8,128)S(1)} %copy-done), custom_call_target="tpu_custom_call" | custom-call | tf_op jit(solution)/shard_map/pallas_call | solution.py:417
Async XLA Ops:
  5.1 36.5 %collective-permute-start = (bf16[2,2,1024,128]{3,2,1,0:T(8,128)(2,1)}, bf16[2,2,1024,128]{3,2,1,0:T(8,128)(2,1)S(1)}, u32[]{:S(2)}, u32[]{:S(2)}) collective-permute-start(bf16[2,2,1024,128]{3,2,1,0:T(8,128)(2,1)} %get-tuple-element.8), channel_id=1, source_target_pairs={{1,0},{2,1},{3,2},{4,3},{5,4},{6,5},{7,6},{8,7},{9,8},{10,9},{11,1... | collective-permute-start | bytes 3145736 | tf_op jit(solution)/shard_map/ppermute | solution.py:444
  6.4 35.2 %collective-permute-start.1 = (bf16[2,2,1024,128]{3,2,1,0:T(8,128)(2,1)}, bf16[2,2,1024,128]{3,2,1,0:T(8,128)(2,1)S(1)}, u32[]{:S(2)}, u32[]{:S(2)}) collective-permute-start(bf16[2,2,1024,128]{3,2,1,0:T(8,128)(2,1)} %get-tuple-element.9), channel_id=1, source_target_pairs={{0,1},{1,2},{2,3},{3,4},{4,5},{5,6},{6,7},{7,8},{8,9},{9,10},{10,1... | collective-permute-start | bytes 3145736 | tf_op jit(solution)/shard_map/ppermute | solution.py:445
  11.0 30.6 %collective-permute-start.2 = (bf16[2,2,1024,128]{3,2,1,0:T(8,128)(2,1)S(1)}, bf16[2,2,1024,128]{3,2,1,0:T(8,128)(2,1)}, u32[]{:S(2)}, u32[]{:S(2)}) collective-permute-start(bf16[2,2,1024,128]{3,2,1,0:T(8,128)(2,1)S(1)} %get-tuple-element.10), channel_id=1, source_target_pairs={{0,16},{16,32},{32,48},{48,64},{64,80},{80,96},{96,112},{1,17},{17... | collective-permute-start | bytes 3145736 | tf_op jit(solution)/shard_map/ppermute | solution.py:446
  41.5 39.9 %copy-start = (s32[2,32,32]{2,1,0:T(8,128)S(1)}, s32[2,32,32]{2,1,0:T(8,128)}, u32[]{:S(2)}) copy-start(s32[2,32,32]{2,1,0:T(8,128)} %adjacency.1) | copy-start | bytes 24580
  60.2 21.2 %all-to-all-start = ((f32[128,1,128]{2,1,0:T(1,128)}), f32[128,1,128]{2,1,0:T(1,128)S(1)}, u32[]{:S(2)}, u32[]{:S(2)}) async-start(f32[128,1,128]{2,1,0:T(1,128)} %bitcast.11), calls=%async_computation | async-start | bytes 131072 | tf_op jit(solution)/shard_map/all_to_all | solution.py:449

commit v4 on v3

--- a/solution.py
+++ b/solution.py
@@ -205,14 +205,20 @@
     table, px, w, below, above, left, inner, out_ref, buffers, tiles, wide, arrived, received, staged
 ):
     n = pl.program_id(0)
-    for step, source in enumerate((below, above, left)):
-
-        @pl.when(n == step)
-        def _(source=source):
-            pltpu.make_async_copy(source, received, staged).start()
+    def stage(source, place):
+        return pltpu.make_async_copy(source, received.at[place], staged.at[place])
+
+    @pl.when(n == 0)
+    def _():
+        stage(below, 0).start()
+        stage(above, 1).start()
+
+    @pl.when(n == 1)
+    def _():
+        stage(left, 0).start()
 
     slot = start_next(OUTER_BATCH, px, w, table, buffers, tiles, arrived)
-    pltpu.make_async_copy(below, received, staged).wait()
+    stage(below, slot).wait()
 
     def steps(sums):
         def finish(pair):
@@ -230,8 +236,8 @@
                 dense = slice(GROUP * v, GROUP * (v + 1))
 
                 own = side_of(tiles.at[slot], wide, pair, pair, entry(table, n, 2 * pair + 1), v)
-                joint = (own * received[pair, 1, dense].astype(F32)).astype(BF16)
-                far = received[pair, 0, dense].astype(F32).astype(I32)
+                joint = (own * received[slot, pair, 1, dense].astype(F32)).astype(BF16)
+                far = received[slot, pair, 0, dense].astype(F32).astype(I32)
                 return (buffers[slot, pair, dense], joint), (far, joint)
 
             strip_products(sums[pair % 2], strips)
@@ -259,8 +265,8 @@
             pltpu.VMEM((2, OUTER_BATCH, LINES, LANES), BF16),
             pltpu.VMEM((OUTER_BATCH, LINES, LANES), F32),
             pltpu.SemaphoreType.DMA((2, OUTER_BATCH, 2)),
-            pltpu.VMEM(below.shape, BF16),
-            pltpu.SemaphoreType.DMA,
+            pltpu.VMEM((2,) + below.shape, BF16),
+            pltpu.SemaphoreType.DMA((2,)),
         ],
         out_shape=jax.ShapeDtypeStruct((2, (len(INNER) + count) * 16, 256), F32),
         compiler_params=pltpu.CompilerParams(vmem_limit_bytes=48 << 20),

time: 84.9 us -> 84.9 us (level)
  no operation moved by 1% of the time
where the time goes in v4:
time: 84.9 us; the launch traced here: 84.7 us
  Pallas kernels  52.9 us (62%)
  starting transfers between devices  21.9 us (26%)
  waiting for transfers between devices  9.71 us (11%)
    pallas_call x1, Pallas kernels, inner_sums(): pl.pallas_call(functools.partial(inner_kernel, INNER.reshape(steps, 4 * B...  25.9 us
    pallas_call x1, Pallas kernels, all_sums(): pl.pallas_call(functools.partial(outer_kernel, OUTER.reshape(count // OUT...  17.3 us
    all_to_all x1, starting transfers between devices, body(): lax.all_to_all(results(sums, count_x * count_y), ALL, 0, 0, tiled=True)  11.4 us
    all_to_all x1, waiting for transfers between devices, body(): lax.all_to_all(results(sums, count_x * count_y), ALL, 0, 0, tiled=True)  9.7 us
    pallas_call x1, Pallas kernels, packed(): pl.pallas_call(pack_kernel, in_specs=[pl.BlockSpec(memory_space=pl.ANY)]...  5.05 us
    ppermute x1, starting transfers between devices, body(): above = lax.ppermute(above, 'gy', ahead(count_y))  4.64 us
    ppermute x1, starting transfers between devices, body(): left = lax.ppermute(left, 'gx', ahead(count_x))  4.57 us
    pallas_call x1, Pallas kernels, sweeps(): pl.pallas_call(functools.partial(sweep_kernel, height, width, height // R...  3.29 us
  transfers between devices with their start and end apart: 4, of which 1 were waited for; matrix products, arithmetic and copies ran while one was open for 0% of the time, Pallas kernels for 31%

profile of v4, /device:TPU:1, one launch (start us, length us, event | category | flops | bytes accessed | tf_op | source)
XLA Modules:
  0.0 84.7 jit_solution(4915091999534492324)
XLA Ops:
  0.0 5.0 %shard_map.37 = (bf16[2,2,1024,128]{3,2,1,0:T(8,128)(2,1)}, bf16[2,2,1024,128]{3,2,1,0:T(8,128)(2,1)}, bf16[2,2,1024,128]{3,2,1,0:T(8,128)(2,1)S(1)}) custom-call(s32[8,1024,4,128]{3,2,1,0:T(4,128)} %bitcast.15, bf16[8,4096,128]{2,1,0:T(8,128)(2,1)} %bitcast.18), custom_call_target="tpu_custom_call" | custom-call | flops 1048576 | bytes 8388608 | tf_op jit(solution)/shard_map/pallas_call | solution.py:132
  5.1 1.3 %collective-permute-start = (bf16[2,2,1024,128]{3,2,1,0:T(8,128)(2,1)}, bf16[2,2,1024,128]{3,2,1,0:T(8,128)(2,1)S(1)}, u32[]{:S(2)}, u32[]{:S(2)}) collective-permute-start(bf16[2,2,1024,128]{3,2,1,0:T(8,128)(2,1)} %get-tuple-element.8), channel_id=1, source_target_pairs={{1,0},{2,1},{3,2},{4,3},{5,4},{6,5},{7,6},{8,7},{9,8},{10,9},{11,1... | collective-permute-start | bytes 3145736 | tf_op jit(solution)/shard_map/ppermute | solution.py:450
  6.4 4.6 %collective-permute-start.1 = (bf16[2,2,1024,128]{3,2,1,0:T(8,128)(2,1)}, bf16[2,2,1024,128]{3,2,1,0:T(8,128)(2,1)S(1)}, u32[]{:S(2)}, u32[]{:S(2)}) collective-permute-start(bf16[2,2,1024,128]{3,2,1,0:T(8,128)(2,1)} %get-tuple-element.9), channel_id=1, source_target_pairs={{0,1},{1,2},{2,3},{3,4},{4,5},{5,6},{6,7},{7,8},{8,9},{9,10},{10,1... | collective-permute-start | bytes 3145736 | tf_op jit(solution)/shard_map/ppermute | solution.py:451
  11.0 4.6 %collective-permute-start.2 = (bf16[2,2,1024,128]{3,2,1,0:T(8,128)(2,1)S(1)}, bf16[2,2,1024,128]{3,2,1,0:T(8,128)(2,1)}, u32[]{:S(2)}, u32[]{:S(2)}) collective-permute-start(bf16[2,2,1024,128]{3,2,1,0:T(8,128)(2,1)S(1)} %get-tuple-element.10), channel_id=1, source_target_pairs={{0,16},{16,32},{32,48},{48,64},{64,80},{80,96},{96,112},{1,17},{17... | collective-permute-start | bytes 3145736 | tf_op jit(solution)/shard_map/ppermute | solution.py:452
  15.6 25.9 %shard_map.38.inner = f32[2,160,256]{2,1,0:T(8,128)S(1)} custom-call(s32[8,1024,4,128]{3,2,1,0:T(4,128)} %bitcast.16, bf16[8,4096,128]{2,1,0:T(8,128)(2,1)} %bitcast.19), custom_call_target="tpu_custom_call" | custom-call | flops 21474836480 | bytes 31457280 | tf_op jit(solution)/shard_map/pallas_call | solution.py:185
  41.5 0.0 copy-start
  41.5 0.0 collective-permute-done.below
  41.6 0.0 collective-permute-done.1.above
  41.6 0.0 collective-permute-done.2.left
  41.6 17.3 %shard_map.39.sums = f32[2,256,256]{2,1,0:T(8,128)S(1)} custom-call(s32[8,1024,4,128]{3,2,1,0:T(4,128)} %bitcast.17, bf16[8,4096,128]{2,1,0:T(8,128)(2,1)} %bitcast.20, bf16[2,2,1024,128]{3,2,1,0:T(8,128)(2,1)S(1)} %collective-permute-done.below, bf16[2,2,1024,128]{3,2,1,0:T(8,128)(2,1)S(1)} %collective-permute-done.1.above, ...), custom_call_target="tpu_custom_call" | custom-call | flops 12884901888 | bytes 9437184 | tf_op jit(solution)/shard_map/pallas_call | solution.py:258
  58.9 1.3 %shard_map.40 = f32[128,128]{1,0:T(8,128)} custom-call(f32[2,256,256]{2,1,0:T(8,128)S(1)} %shard_map.39.sums), custom_call_target="tpu_custom_call" | custom-call | tf_op jit(solution)/shard_map/pallas_call | solution.py:332
  60.2 11.4 %all-to-all-start = ((f32[128,1,128]{2,1,0:T(1,128)}), f32[128,1,128]{2,1,0:T(1,128)S(1)}, u32[]{:S(2)}, u32[]{:S(2)}) async-start(f32[128,1,128]{2,1,0:T(1,128)} %bitcast.11), calls=%async_computation | async-start | bytes 131072 | tf_op jit(solution)/shard_map/all_to_all | solution.py:455
  71.6 0.1 pad_add_fusion.where_ref
  71.7 9.7 %all-to-all-done = f32[128,1,128]{2,1,0:T(1,128)S(1)} async-done(((f32[128,1,128]{2,1,0:T(1,128)}), f32[128,1,128]{2,1,0:T(1,128)S(1)}, u32[]{:S(2)}, u32[]{:S(2)}) %all-to-all-start) | async-done | bytes 65568 | tf_op jit(solution)/shard_map/all_to_all | solution.py:455
  81.4 0.0 copy-done
  81.4 3.3 %shard_map.41 = f32[2,4]{1,0:T(2,128)} custom-call(s32[2]{0:T(128)S(1)} %pad_add_fusion.where_ref, f32[128,128]{1,0:T(8,128)S(1)} %bitcast.14, s32[2,32,32]{2,1,0:T(8,128)S(1)} %copy-done), custom_call_target="tpu_custom_call" | custom-call | tf_op jit(solution)/shard_map/pallas_call | solution.py:423
Async XLA Ops:
  5.1 36.5 %collective-permute-start = (bf16[2,2,1024,128]{3,2,1,0:T(8,128)(2,1)}, bf16[2,2,1024,128]{3,2,1,0:T(8,128)(2,1)S(1)}, u32[]{:S(2)}, u32[]{:S(2)}) collective-permute-start(bf16[2,2,1024,128]{3,2,1,0:T(8,128)(2,1)} %get-tuple-element.8), channel_id=1, source_target_pairs={{1,0},{2,1},{3,2},{4,3},{5,4},{6,5},{7,6},{8,7},{9,8},{10,9},{11,1... | collective-permute-start | bytes 3145736 | tf_op jit(solution)/shard_map/ppermute | solution.py:450
  6.4 35.2 %collective-permute-start.1 = (bf16[2,2,1024,128]{3,2,1,0:T(8,128)(2,1)}, bf16[2,2,1024,128]{3,2,1,0:T(8,128)(2,1)S(1)}, u32[]{:S(2)}, u32[]{:S(2)}) collective-permute-start(bf16[2,2,1024,128]{3,2,1,0:T(8,128)(2,1)} %get-tuple-element.9), channel_id=1, source_target_pairs={{0,1},{1,2},{2,3},{3,4},{4,5},{5,6},{6,7},{7,8},{8,9},{9,10},{10,1... | collective-permute-start | bytes 3145736 | tf_op jit(solution)/shard_map/ppermute | solution.py:451
  11.0 30.6 %collective-permute-start.2 = (bf16[2,2,1024,128]{3,2,1,0:T(8,128)(2,1)S(1)}, bf16[2,2,1024,128]{3,2,1,0:T(8,128)(2,1)}, u32[]{:S(2)}, u32[]{:S(2)}) collective-permute-start(bf16[2,2,1024,128]{3,2,1,0:T(8,128)(2,1)S(1)} %get-tuple-element.10), channel_id=1, source_target_pairs={{0,16},{16,32},{32,48},{48,64},{64,80},{80,96},{96,112},{1,17},{17... | collective-permute-start | bytes 3145736 | tf_op jit(solution)/shard_map/ppermute | solution.py:452
  41.5 39.9 %copy-start = (s32[2,32,32]{2,1,0:T(8,128)S(1)}, s32[2,32,32]{2,1,0:T(8,128)}, u32[]{:S(2)}) copy-start(s32[2,32,32]{2,1,0:T(8,128)} %adjacency.1) | copy-start | bytes 24580
  60.2 21.2 %all-to-all-start = ((f32[128,1,128]{2,1,0:T(1,128)}), f32[128,1,128]{2,1,0:T(1,128)S(1)}, u32[]{:S(2)}, u32[]{:S(2)}) async-start(f32[128,1,128]{2,1,0:T(1,128)} %bitcast.11), calls=%async_computation | async-start | bytes 131072 | tf_op jit(solution)/shard_map/all_to_all | solution.py:455

commit v5 on v3

--- a/solution.py
+++ b/solution.py
@@ -13,7 +13,7 @@
 CHUNKS, LANES = 1024, 128
 LINES = 4 * CHUNKS
 BATCH = 2
-OUTER_BATCH = 2
+OUTER_BATCH = 6
 GROUP = 16
 ALL = ("gx", "gy")
 F32, BF16, I32 = jnp.float32, jnp.bfloat16, jnp.int32
@@ -202,25 +202,18 @@
 
 
 def outer_kernel(
-    table, px, w, below, above, left, inner, out_ref, buffers, tiles, wide, arrived, received, staged
+    table, px, w, below, above, left, inner, out_ref, buffers, tiles, wide, arrived
 ):
     n = pl.program_id(0)
-    for step, source in enumerate((below, above, left)):
-
-        @pl.when(n == step)
-        def _(source=source):
-            pltpu.make_async_copy(source, received, staged).start()
-
     slot = start_next(OUTER_BATCH, px, w, table, buffers, tiles, arrived)
-    pltpu.make_async_copy(below, received, staged).wait()
 
     def steps(sums):
         def finish(pair):
             own, other = (diagonal_sum(pltpu.matmul_pop(sums[pair % 2][place])) for place in range(2))
             at = len(INNER) + OUTER_BATCH * n + pair
             rows = pl.ds(pl.multiple_of(at * 16, 16), 16)
-            out_ref[0, rows] = jnp.where(n == 0, own, other)
-            out_ref[1, rows] = jnp.where(n == 0, other, own)
+            out_ref[0, rows] = own if pair < 2 else other
+            out_ref[1, rows] = other if pair < 2 else own
 
         for pair in range(OUTER_BATCH):
             for copy in fetch(px, w, table, n, buffers, tiles, arrived, slot, pair):
@@ -229,9 +222,9 @@
             def strips(v):
                 dense = slice(GROUP * v, GROUP * (v + 1))
 
-                own = side_of(tiles.at[slot], wide, pair, pair, entry(table, n, 2 * pair + 1), v)
-                joint = (own * received[pair, 1, dense].astype(F32)).astype(BF16)
-                far = received[pair, 0, dense].astype(F32).astype(I32)
+                own = side_of(tiles.at[slot], wide, pair, pair % 2, entry(table, n, 2 * pair + 1), v)
+                joint = (own * (below, above, left)[pair // 2][pair % 2, 1, dense].astype(F32)).astype(BF16)
+                far = (below, above, left)[pair // 2][pair % 2, 0, dense].astype(F32).astype(I32)
                 return (buffers[slot, pair, dense], joint), (far, joint)
 
             strip_products(sums[pair % 2], strips)
@@ -257,10 +250,8 @@
         scratch_shapes=[
             pltpu.VMEM((2, OUTER_BATCH, CHUNKS, LANES), I32),
             pltpu.VMEM((2, OUTER_BATCH, LINES, LANES), BF16),
-            pltpu.VMEM((OUTER_BATCH, LINES, LANES), F32),
+            pltpu.VMEM((2, LINES, LANES), F32),
             pltpu.SemaphoreType.DMA((2, OUTER_BATCH, 2)),
-            pltpu.VMEM(below.shape, BF16),
-            pltpu.SemaphoreType.DMA,
         ],
         out_shape=jax.ShapeDtypeStruct((2, (len(INNER) + count) * 16, 256), F32),
         compiler_params=pltpu.CompilerParams(vmem_limit_bytes=48 << 20),

time: 84.9 us -> 85.1 us (level)
  no operation moved by 1% of the time
where the time goes in v5:
time: 85.1 us; the launch traced here: 84.9 us
  Pallas kernels  52.9 us (62%)
  starting transfers between devices  21.9 us (26%)
  waiting for transfers between devices  9.71 us (11%)
    pallas_call x1, Pallas kernels, inner_sums(): pl.pallas_call(functools.partial(inner_kernel, INNER.reshape(steps, 4 * B...  26.1 us
    pallas_call x1, Pallas kernels, all_sums(): pl.pallas_call(functools.partial(outer_kernel, OUTER.reshape(count // OUT...  17.1 us
    all_to_all x1, starting transfers between devices, body(): lax.all_to_all(results(sums, count_x * count_y), ALL, 0, 0, tiled=True)  11.4 us
    all_to_all x1, waiting for transfers between devices, body(): lax.all_to_all(results(sums, count_x * count_y), ALL, 0, 0, tiled=True)  9.7 us
    pallas_call x1, Pallas kernels, packed(): pl.pallas_call(pack_kernel, in_specs=[pl.BlockSpec(memory_space=pl.ANY)]...  5.05 us
    ppermute x1, starting transfers between devices, body(): above = lax.ppermute(above, 'gy', ahead(count_y))  4.64 us
    ppermute x1, starting transfers between devices, body(): left = lax.ppermute(left, 'gx', ahead(count_x))  4.57 us
    pallas_call x1, Pallas kernels, sweeps(): pl.pallas_call(functools.partial(sweep_kernel, height, width, height // R...  3.29 us
  transfers between devices with their start and end apart: 4, of which 1 were waited for; matrix products, arithmetic and copies ran while one was open for 0% of the time, Pallas kernels for 31%

profile of v5, /device:TPU:1, one launch (start us, length us, event | category | flops | bytes accessed | tf_op | source)
XLA Modules:
  0.0 84.9 jit_solution(10631140042635360954)
XLA Ops:
  0.0 5.0 %shard_map.37 = (bf16[2,2,1024,128]{3,2,1,0:T(8,128)(2,1)}, bf16[2,2,1024,128]{3,2,1,0:T(8,128)(2,1)}, bf16[2,2,1024,128]{3,2,1,0:T(8,128)(2,1)S(1)}) custom-call(s32[8,1024,4,128]{3,2,1,0:T(4,128)} %bitcast.15, bf16[8,4096,128]{2,1,0:T(8,128)(2,1)} %bitcast.18), custom_call_target="tpu_custom_call" | custom-call | flops 1048576 | bytes 8388608 | tf_op jit(solution)/shard_map/pallas_call | solution.py:132
  5.1 1.3 %collective-permute-start = (bf16[2,2,1024,128]{3,2,1,0:T(8,128)(2,1)}, bf16[2,2,1024,128]{3,2,1,0:T(8,128)(2,1)S(1)}, u32[]{:S(2)}, u32[]{:S(2)}) collective-permute-start(bf16[2,2,1024,128]{3,2,1,0:T(8,128)(2,1)} %get-tuple-element.8), channel_id=1, source_target_pairs={{1,0},{2,1},{3,2},{4,3},{5,4},{6,5},{7,6},{8,7},{9,8},{10,9},{11,1... | collective-permute-start | bytes 3145736 | tf_op jit(solution)/shard_map/ppermute | solution.py:435
  6.4 4.6 %collective-permute-start.1 = (bf16[2,2,1024,128]{3,2,1,0:T(8,128)(2,1)}, bf16[2,2,1024,128]{3,2,1,0:T(8,128)(2,1)S(1)}, u32[]{:S(2)}, u32[]{:S(2)}) collective-permute-start(bf16[2,2,1024,128]{3,2,1,0:T(8,128)(2,1)} %get-tuple-element.9), channel_id=1, source_target_pairs={{0,1},{1,2},{2,3},{3,4},{4,5},{5,6},{6,7},{7,8},{8,9},{9,10},{10,1... | collective-permute-start | bytes 3145736 | tf_op jit(solution)/shard_map/ppermute | solution.py:436
  11.0 4.6 %collective-permute-start.2 = (bf16[2,2,1024,128]{3,2,1,0:T(8,128)(2,1)S(1)}, bf16[2,2,1024,128]{3,2,1,0:T(8,128)(2,1)}, u32[]{:S(2)}, u32[]{:S(2)}) collective-permute-start(bf16[2,2,1024,128]{3,2,1,0:T(8,128)(2,1)S(1)} %get-tuple-element.10), channel_id=1, source_target_pairs={{0,16},{16,32},{32,48},{48,64},{64,80},{80,96},{96,112},{1,17},{17... | collective-permute-start | bytes 3145736 | tf_op jit(solution)/shard_map/ppermute | solution.py:437
  15.6 26.1 %shard_map.38.inner = f32[2,160,256]{2,1,0:T(8,128)S(1)} custom-call(s32[8,1024,4,128]{3,2,1,0:T(4,128)} %bitcast.16, bf16[8,4096,128]{2,1,0:T(8,128)(2,1)} %bitcast.19), custom_call_target="tpu_custom_call" | custom-call | flops 21474836480 | bytes 31457280 | tf_op jit(solution)/shard_map/pallas_call | solution.py:185
  41.7 0.0 copy-start
  41.7 0.0 collective-permute-done.below
  41.7 0.0 collective-permute-done.1.above
  41.8 0.0 collective-permute-done.2.left
  41.8 17.1 %shard_map.39.sums = f32[2,256,256]{2,1,0:T(8,128)S(1)} custom-call(s32[8,1024,4,128]{3,2,1,0:T(4,128)} %bitcast.17, bf16[8,4096,128]{2,1,0:T(8,128)(2,1)} %bitcast.20, bf16[2,2,1024,128]{3,2,1,0:T(8,128)(2,1)S(1)} %collective-permute-done.below, bf16[2,2,1024,128]{3,2,1,0:T(8,128)(2,1)S(1)} %collective-permute-done.1.above, ...), custom_call_target="tpu_custom_call" | custom-call | flops 12884901888 | bytes 9437184 | tf_op jit(solution)/shard_map/pallas_call | solution.py:245
  58.9 1.3 %shard_map.40 = f32[128,128]{1,0:T(8,128)} custom-call(f32[2,256,256]{2,1,0:T(8,128)S(1)} %shard_map.39.sums), custom_call_target="tpu_custom_call" | custom-call | tf_op jit(solution)/shard_map/pallas_call | solution.py:317
  60.2 11.4 %all-to-all-start = ((f32[128,1,128]{2,1,0:T(1,128)}), f32[128,1,128]{2,1,0:T(1,128)S(1)}, u32[]{:S(2)}, u32[]{:S(2)}) async-start(f32[128,1,128]{2,1,0:T(1,128)} %bitcast.11), calls=%async_computation | async-start | bytes 131072 | tf_op jit(solution)/shard_map/all_to_all | solution.py:440
  71.7 0.1 pad_add_fusion.where_ref
  71.8 9.7 %all-to-all-done = f32[128,1,128]{2,1,0:T(1,128)S(1)} async-done(((f32[128,1,128]{2,1,0:T(1,128)}), f32[128,1,128]{2,1,0:T(1,128)S(1)}, u32[]{:S(2)}, u32[]{:S(2)}) %all-to-all-start) | async-done | bytes 65568 | tf_op jit(solution)/shard_map/all_to_all | solution.py:440
  81.5 0.0 copy-done
  81.5 3.3 %shard_map.41 = f32[2,4]{1,0:T(2,128)} custom-call(s32[2]{0:T(128)S(1)} %pad_add_fusion.where_ref, f32[128,128]{1,0:T(8,128)S(1)} %bitcast.14, s32[2,32,32]{2,1,0:T(8,128)S(1)} %copy-done), custom_call_target="tpu_custom_call" | custom-call | tf_op jit(solution)/shard_map/pallas_call | solution.py:408
Async XLA Ops:
  5.1 36.7 %collective-permute-start = (bf16[2,2,1024,128]{3,2,1,0:T(8,128)(2,1)}, bf16[2,2,1024,128]{3,2,1,0:T(8,128)(2,1)S(1)}, u32[]{:S(2)}, u32[]{:S(2)}) collective-permute-start(bf16[2,2,1024,128]{3,2,1,0:T(8,128)(2,1)} %get-tuple-element.8), channel_id=1, source_target_pairs={{1,0},{2,1},{3,2},{4,3},{5,4},{6,5},{7,6},{8,7},{9,8},{10,9},{11,1... | collective-permute-start | bytes 3145736 | tf_op jit(solution)/shard_map/ppermute | solution.py:435
  6.4 35.4 %collective-permute-start.1 = (bf16[2,2,1024,128]{3,2,1,0:T(8,128)(2,1)}, bf16[2,2,1024,128]{3,2,1,0:T(8,128)(2,1)S(1)}, u32[]{:S(2)}, u32[]{:S(2)}) collective-permute-start(bf16[2,2,1024,128]{3,2,1,0:T(8,128)(2,1)} %get-tuple-element.9), channel_id=1, source_target_pairs={{0,1},{1,2},{2,3},{3,4},{4,5},{5,6},{6,7},{7,8},{8,9},{9,10},{10,1... | collective-permute-start | bytes 3145736 | tf_op jit(solution)/shard_map/ppermute | solution.py:436
  11.0 30.8 %collective-permute-start.2 = (bf16[2,2,1024,128]{3,2,1,0:T(8,128)(2,1)S(1)}, bf16[2,2,1024,128]{3,2,1,0:T(8,128)(2,1)}, u32[]{:S(2)}, u32[]{:S(2)}) collective-permute-start(bf16[2,2,1024,128]{3,2,1,0:T(8,128)(2,1)S(1)} %get-tuple-element.10), channel_id=1, source_target_pairs={{0,16},{16,32},{32,48},{48,64},{64,80},{80,96},{96,112},{1,17},{17... | collective-permute-start | bytes 3145736 | tf_op jit(solution)/shard_map/ppermute | solution.py:437
  41.7 39.7 %copy-start = (s32[2,32,32]{2,1,0:T(8,128)S(1)}, s32[2,32,32]{2,1,0:T(8,128)}, u32[]{:S(2)}) copy-start(s32[2,32,32]{2,1,0:T(8,128)} %adjacency.1) | copy-start | bytes 24580
  60.2 21.2 %all-to-all-start = ((f32[128,1,128]{2,1,0:T(1,128)}), f32[128,1,128]{2,1,0:T(1,128)S(1)}, u32[]{:S(2)}, u32[]{:S(2)}) async-start(f32[128,1,128]{2,1,0:T(1,128)} %bitcast.11), calls=%async_computation | async-start | bytes 131072 | tf_op jit(solution)/shard_map/all_to_all | solution.py:440
